TPU v7x, 512 devices: a whole 4x4x16 slice. The times are simulated.
512 devices in a mesh: outer: 64 (over z_lo, y, x), inner: 8 (over z_hi, core).
Axes of the slice: x: 4, y: 4, z: 16 (z_hi: 4, z_lo: 4; z = z_hi * 4 + z_lo), core: 2. Of those that a mesh axis runs over, the one named last changes fastest.
Arguments:
- queries: bfloat16 [65536, 2048], P(('outer', 'inner')), may hold values from -6 to 6
- keys: bfloat16 [65536, 2048], P(('outer', 'inner')), may hold values from -6 to 6
- values: bfloat16 [65536, 2048], P(('outer', 'inner')), may hold values from -6 to 6
- grad_out: bfloat16 [65536, 2048], P(('outer', 'inner')), may hold values from -48 to 48
- lse: bfloat16 [65536, 16], P(('outer', 'inner')), may hold values from 4 to 7
- delta: bfloat16 [65536, 16], P(('outer', 'inner')), may hold values from -360 to 360
- span_table: int32 [512, 2], replicated, may hold values from 0 to 1023, as said below
Outputs:
- grad_queries: float32 [65536, 2048], P(('outer', 'inner'))
- grad_keys: float32 [65536, 2048], P(('outer', 'inner'))
- grad_values: float32 [65536, 2048], P(('outer', 'inner'))
Inputs may be any that keep to these rules, and one draw needn't show every extreme that they name: `span_table`: row d is (c, 1023 - c); the first column is a permutation of 0 to 511.
All inputs are finite; a program needn't handle non-finite values.
Results may differ from a plain program's by a relative error of at most 0.014.
Values may be sent and summed in bfloat16 or wider, within the bound.
No kernel may reach another device: no remote copies, remote signals or barrier semaphores. Data moves between devices by JAX's collectives and lax.ppermute only.
A program may use at most 64 MiB of HBM per device.

v0:
```python
import jax
import jax.numpy as jnp
from jax import lax
from jax.sharding import PartitionSpec as P


def passed_along(x, axis, by):
    count = lax.axis_size(axis)
    return lax.ppermute(x, axis, [(i, (i + by) % count) for i in range(count)])


def token_positions(table, half):
    flat = table.reshape(-1)
    spread = jnp.broadcast_to(flat[:, None], (flat.shape[0], half)) * half
    return (spread + jnp.arange(half, dtype=jnp.int32)[None, :]).reshape(-1)


def group_work(key_rows, value_rows, key_pos, queries, grad_out, lse, delta, group_table):
    half = queries.shape[0] // 2
    q_all, o_all, l_all, d_all = (
        lax.all_gather(queries, "inner", axis=0, tiled=True),
        lax.all_gather(grad_out, "inner", axis=0, tiled=True),
        lax.all_gather(lse, "inner", axis=0, tiled=True),
        lax.all_gather(delta, "inner", axis=0, tiled=True),
    )
    query_pos = token_positions(group_table, half)
    rows = q_all.shape[0]
    heads = lse.shape[1]
    width = queries.shape[1] // heads
    shard = key_rows.shape[0]
    scale = width ** (-0.5)
    q3 = q_all.reshape(rows, heads, width)
    o3 = o_all.reshape(rows, heads, width)
    k3 = key_rows.reshape(shard, heads, width)
    v3 = value_rows.reshape(shard, heads, width)
    lse_t = l_all.astype(jnp.float32).T
    delta_t = d_all.astype(jnp.float32).T
    allowed = key_pos[None, :] <= query_pos[:, None]
    block = 4
    count = heads // block

    def head_block(step, carry):
        terms, grad_k, grad_v = carry
        start = step * block
        qb = lax.dynamic_slice_in_dim(q3, start, block, 1)
        ob = lax.dynamic_slice_in_dim(o3, start, block, 1)
        kb = lax.dynamic_slice_in_dim(k3, start, block, 1)
        vb = lax.dynamic_slice_in_dim(v3, start, block, 1)
        lb = lax.dynamic_slice_in_dim(lse_t, start, block, 0)
        db = lax.dynamic_slice_in_dim(delta_t, start, block, 0)
        scores = jnp.einsum("qhd,khd->hqk", qb, kb, preferred_element_type=jnp.float32)
        probs = jnp.where(allowed[None], jnp.exp(scores * scale - lb[:, :, None]), 0.0)
        dv_block = jnp.einsum(
            "hqk,qhd->khd", probs.astype(jnp.bfloat16), ob, preferred_element_type=jnp.float32
        )
        dprob = jnp.einsum("qhd,khd->hqk", ob, vb, preferred_element_type=jnp.float32)
        dscore = (probs * (dprob - db[:, :, None])).astype(jnp.bfloat16)
        dq_block = scale * jnp.einsum(
            "hqk,khd->qhd", dscore, kb, preferred_element_type=jnp.float32
        )
        dk_block = scale * jnp.einsum(
            "hqk,qhd->khd", dscore, qb, preferred_element_type=jnp.float32
        )
        terms = lax.dynamic_update_slice_in_dim(terms, dq_block, start, 1)
        grad_k = lax.dynamic_update_slice_in_dim(grad_k, dk_block, start, 1)
        grad_v = lax.dynamic_update_slice_in_dim(grad_v, dv_block, start, 1)
        return (terms, grad_k, grad_v)

    start_carry = (
        jnp.zeros((rows, heads, width), jnp.float32),
        jnp.zeros((shard, heads, width), jnp.float32),
        jnp.zeros((shard, heads, width), jnp.float32),
    )
    terms, grad_k, grad_v = lax.fori_loop(0, count, head_block, start_carry)
    grad_q = lax.psum_scatter(
        terms.reshape(rows, heads * width).astype(jnp.bfloat16),
        "inner",
        scatter_dimension=0,
        tiled=True,
    ).astype(jnp.float32)
    return (grad_q, grad_k.reshape(shard, heads * width), grad_v.reshape(shard, heads * width))


def shards(queries, keys, values, grad_out, lse, delta, span_table):
    outer_count = lax.axis_size("outer")
    inner_count = lax.axis_size("inner")
    outer_idx = lax.axis_index("outer")
    inner_idx = lax.axis_index("inner")
    half = queries.shape[0] // 2
    remote_k, remote_v = passed_along((keys, values), "outer", 1)
    source = (outer_idx + outer_count - 1) % outer_count
    key_table = lax.dynamic_slice_in_dim(span_table, source * inner_count + inner_idx, 1, 0)
    group_table = lax.dynamic_slice_in_dim(span_table, outer_idx * inner_count, inner_count, 0)
    grad_q, remote_gk, remote_gv = group_work(
        remote_k,
        remote_v,
        token_positions(key_table, half),
        queries,
        grad_out,
        lse,
        delta,
        group_table,
    )
    grad_k, grad_v = (
        passed_along(remote_gk.astype(jnp.bfloat16), "outer", -1).astype(remote_gk.dtype),
        passed_along(remote_gv.astype(jnp.bfloat16), "outer", -1).astype(remote_gv.dtype),
    )
    return (grad_q, grad_k, grad_v)


def solution(mesh):
    placed = (
        P(("outer", "inner"), None),
        P(("outer", "inner"), None),
        P(("outer", "inner"), None),
        P(("outer", "inner"), None),
        P(("outer", "inner"), None),
        P(("outer", "inner"), None),
        P(),
    )
    return jax.shard_map(
        shards,
        mesh=mesh,
        in_specs=placed,
        out_specs=(
            P(("outer", "inner"), None),
            P(("outer", "inner"), None),
            P(("outer", "inner"), None),
        ),
        check_vma=False,
    )
```

profile of v0, /device:TPU:64, one launch (start us, length us, event | category | flops | bytes accessed | tf_op | source)
XLA Modules:
  0.0 410.6 jit_solution(13270281947128032828)
XLA Ops:
  7.2 2.1 copy.21
  9.4 2.0 copy.22
  11.6 0.3 copy.23
  11.8 3.4 collective-permute-start.1
  15.2 0.3 copy.20
  15.5 3.4 collective-permute-start
  19.7 28.8 %all_gather.13 = bf16[1024,16]{0,1:T(8,128)(2,1)S(1)} all-gather(bf16[128,16]{0,1:T(8,128)(2,1)S(1)} %copy-done.4), channel_id=1, replica_groups=mesh['outer'=64,'inner'=8] {'inner'}, dimensions={0}, use_global_device_ids=true | all-gather | bytes 36864 | tf_op jit(solution)/shard_map/all_gather | solution.py:23
  48.5 26.9 %all_gather.15 = bf16[1024,16]{0,1:T(8,128)(2,1)S(1)} all-gather(bf16[128,16]{0,1:T(8,128)(2,1)S(1)} %copy-done.5), channel_id=1, replica_groups=mesh['outer'=64,'inner'=8] {'inner'}, dimensions={0}, use_global_device_ids=true | all-gather | bytes 36864 | tf_op jit(solution)/shard_map/all_gather | solution.py:24
  75.4 32.9 %all-gather.3.cloned.1.call-done = bf16[1024,2048]{0,1:T(8,128)(2,1)} async-done(((bf16[128,2048]{0,1:T(8,128)(2,1)}), bf16[1024,2048]{0,1:T(8,128)(2,1)}) %all-gather.3.cloned.1.call-update) | async-done | bytes 4194320 | tf_op jit(solution)/shard_map/all_gather | solution.py:21
  108.3 114.9 %all-gather.5.cloned.1.call-done = bf16[1024,2048]{0,1:T(8,128)(2,1)} async-done(((bf16[128,2048]{0,1:T(8,128)(2,1)}), bf16[1024,2048]{0,1:T(8,128)(2,1)}) %all-gather.5.cloned.1.call-update) | async-done | bytes 4194320 | tf_op jit(solution)/shard_map/all_gather | solution.py:22
  223.4 2.5 broadcast_in_dim.48
  225.9 42.3 %while.18 = (s32[]{:T(128)}, bf16[1024,16,128]{0,2,1:T(8,128)(2,1)}, bf16[128,16,128]{0,2,1:T(8,128)(2,1)S(1)}, bf16[128,16,128]{0,2,1:T(8,128)(2,1)S(1)}, bf16[...) while((s32[]{:T(128)}, ...), condition=%wide.region_1.2_spmd.clone, body=%wide.region_0.1_spmd.clone.sunk | while | flops 675479552 | bytes 50571004 | solution.py:74
  225.9 0.2 broadcast_compare_fusion.2
  226.1 2.1 exponential_select_fusion.2
  228.3 1.7 fusion.43
  230.0 2.3 multiply_convert_fusion.2
  232.3 1.7 fusion.42
  234.1 0.4 bitcast_dynamic-update-slice_fusion.2
  234.5 2.0 copy-done.1
  236.7 2.1 exponential_select_fusion.2
  238.8 1.7 fusion.43
  240.6 2.3 multiply_convert_fusion.2
  242.9 1.7 fusion.42
  244.6 0.4 bitcast_dynamic-update-slice_fusion.2
  245.1 2.0 copy-done.1
  247.3 2.1 exponential_select_fusion.2
  249.4 1.7 fusion.43
  251.1 2.3 multiply_convert_fusion.2
  253.5 1.7 fusion.42
  255.2 0.4 bitcast_dynamic-update-slice_fusion.2
  255.7 2.0 copy-done.1
  257.8 2.1 exponential_select_fusion.2
  260.0 1.7 fusion.43
  261.7 2.3 multiply_convert_fusion.2
  264.0 1.7 fusion.42
  265.8 0.4 bitcast_dynamic-update-slice_fusion.2
  266.2 2.0 copy-done.1
  268.2 6.6 %copy.35 = bf16[1024,2048]{1,0:T(8,128)(2,1)} copy(bf16[1024,2048]{0,1:T(8,128)(2,1)} %bitcast.34) | data formatting | bytes 8388608 | tf_op jit(solution)/shard_map/convert_element_type | solution.py:76
  274.8 0.2 copy.36
  275.0 2.6 collective-permute-start.2
  277.6 0.2 copy.37
  277.9 2.9 collective-permute-start.3
  280.8 10.9 %collective-permute-done.2 = bf16[128,2048]{1,0:T(8,128)(2,1)S(1)} collective-permute-done((bf16[128,2048]{1,0:T(8,128)(2,1)S(1)}, bf16[128,2048]{1,0:T(8,128)(2,1)S(1)}, u32[]{:S(2)}, u32[]{:S(2)}) %collective-permute-start.2) | collective-permute-done | bytes 524320 | tf_op jit(solution)/shard_map/ppermute | solution.py:9
  291.6 1.1 convert_element_type.48
  292.7 21.1 %collective-permute-done.3 = bf16[128,2048]{1,0:T(8,128)(2,1)S(1)} collective-permute-done((bf16[128,2048]{1,0:T(8,128)(2,1)S(1)}, bf16[128,2048]{1,0:T(8,128)(2,1)S(1)}, u32[]{:S(2)}, u32[]{:S(2)}) %collective-permute-start.3) | collective-permute-done | bytes 524320 | tf_op jit(solution)/shard_map/ppermute | solution.py:9
  313.8 1.1 convert_element_type.51
  314.9 87.1 %reduce-scatter.2.cloned.1.call-done = bf16[128,2048]{1,0:T(8,128)(2,1)} async-done(((bf16[1024,2048]{1,0:T(8,128)(2,1)}), bf16[128,2048]{1,0:T(8,128)(2,1)}) %reduce-scatter.2.cloned.1.call-update) | async-done | bytes 524304 | tf_op jit(solution)/shard_map/reduce_scatter | solution.py:75
  402.0 2.1 convert_element_type.45
  (49 shorter events, 1.8 us)
Async XLA Ops:
  7.2 4.4 %copy-start.2 = (bf16[128,2048]{1,0:T(8,128)(2,1)S(1)}, bf16[128,2048]{1,0:T(8,128)(2,1)}, u32[]{:S(2)}) copy-start(bf16[128,2048]{1,0:T(8,128)(2,1)} %param.11) | copy-start | bytes 1572868
  7.2 8.1 %copy-start.3 = (bf16[128,2048]{1,0:T(8,128)(2,1)S(1)}, bf16[128,2048]{1,0:T(8,128)(2,1)}, u32[]{:S(2)}) copy-start(bf16[128,2048]{1,0:T(8,128)(2,1)} %param.10) | copy-start | bytes 1572868
  7.2 101.1 %all-gather.3.cloned.1.call-start = ((), (), s32[]{:S(2)}) async-start(), calls=%async_computation.1 | async-start | bytes 4718592 | tf_op jit(solution)/shard_map/all_gather | solution.py:21
  9.3 9.6 %copy-start.6 = (s32[512,2]{0,1:T(2,128)S(1)}, s32[512,2]{0,1:T(2,128)}, u32[]{:S(2)}) copy-start(s32[512,2]{0,1:T(2,128)} %param.15) | copy-start | bytes 12292
  9.4 10.3 %copy-start.4 = (bf16[128,16]{0,1:T(8,128)(2,1)S(1)}, bf16[128,16]{0,1:T(8,128)(2,1)}, u32[]{:S(2)}) copy-start(bf16[128,16]{0,1:T(8,128)(2,1)} %param.13) | copy-start | bytes 12292
  9.4 39.2 %copy-start.5 = (bf16[128,16]{0,1:T(8,128)(2,1)S(1)}, bf16[128,16]{0,1:T(8,128)(2,1)}, u32[]{:S(2)}) copy-start(bf16[128,16]{0,1:T(8,128)(2,1)} %param.14) | copy-start | bytes 12292
  9.4 213.8 %all-gather.5.cloned.1.call-start = ((), (), s32[]{:S(2)}) async-start(), calls=%async_computation.2 | async-start | bytes 4718592 | tf_op jit(solution)/shard_map/all_gather | solution.py:22
  11.5 390.5 %reduce-scatter.2.cloned.1.call-start = ((), (), s32[]{:S(2)}) async-start(), calls=%async_computation.3 | async-start | bytes 4718592 | tf_op jit(solution)/shard_map/reduce_scatter | solution.py:75
  11.8 63.6 %collective-permute-start.1 = (bf16[128,2048]{0,1:T(8,128)(2,1)S(1)}, bf16[128,2048]{0,1:T(8,128)(2,1)S(1)}, u32[]{:S(2)}, u32[]{:S(2)}) collective-permute-start(bf16[128,2048]{0,1:T(8,128)(2,1)S(1)} %copy.23), channel_id=1, source_target_pairs={{0,8},{8,16},{16,24},{24,32},{32,40},{40,48},{48,56},{56,64},{64,7... | collective-permute-start | bytes 1572872 | tf_op jit(solution)/shard_map/ppermute | solution.py:9
  15.5 59.9 %collective-permute-start = (bf16[128,2048]{0,1:T(8,128)(2,1)S(1)}, bf16[128,2048]{0,1:T(8,128)(2,1)S(1)}, u32[]{:S(2)}, u32[]{:S(2)}) collective-permute-start(bf16[128,2048]{0,1:T(8,128)(2,1)S(1)} %copy.20), channel_id=1, source_target_pairs={{0,8},{8,16},{16,24},{24,32},{32,40},{40,48},{48,56},{56,64},{64,7... | collective-permute-start | bytes 1572872 | tf_op jit(solution)/shard_map/ppermute | solution.py:9
  230.0 4.1 copy-start
  234.5 2.0 copy-start.1
  240.6 4.1 copy-start
  245.1 2.0 copy-start.1
  251.1 4.1 copy-start
  255.6 2.0 copy-start.1
  261.7 4.1 copy-start
  266.2 2.0 copy-start.1
  275.0 16.6 %collective-permute-start.2 = (bf16[128,2048]{1,0:T(8,128)(2,1)S(1)}, bf16[128,2048]{1,0:T(8,128)(2,1)S(1)}, u32[]{:S(2)}, u32[]{:S(2)}) collective-permute-start(bf16[128,2048]{1,0:T(8,128)(2,1)S(1)} %copy.36), channel_id=1, source_target_pairs={{0,504},{8,0},{16,8},{24,16},{32,24},{40,32},{48,40},{56,48},{64,5... | collective-permute-start | bytes 1572872 | tf_op jit(solution)/shard_map/ppermute | solution.py:9
  277.9 35.9 %collective-permute-start.3 = (bf16[128,2048]{1,0:T(8,128)(2,1)S(1)}, bf16[128,2048]{1,0:T(8,128)(2,1)S(1)}, u32[]{:S(2)}, u32[]{:S(2)}) collective-permute-start(bf16[128,2048]{1,0:T(8,128)(2,1)S(1)} %copy.37), channel_id=1, source_target_pairs={{0,504},{8,0},{16,8},{24,16},{32,24},{40,32},{48,40},{56,48},{64,5... | collective-permute-start | bytes 1572872 | tf_op jit(solution)/shard_map/ppermute | solution.py:9
Sparse Core Ops, SparseCore 0:
  10.7 97.5 all-gather.2
  111.0 112.1 all-gather.4
  274.9 127.0 reduce-scatter.1
where the time goes:
time: 411 us
  waiting for transfers between devices  267 us (65%)
  blocking collectives  55.7 us (14%)
  matrix products  33.3 us (8%)
  local copies, waits for them, and re-layouts  22.6 us (5%)
  between operations  13.9 us (3%)
  starting transfers between devices  12.5 us (3%)
  other arithmetic  5.5 us (1%)
    all_gather x1, waiting for transfers between devices, group_work(): lax.all_gather(grad_out, 'inner', axis=0, tiled=True)  115 us
    reduce_scatter x1, waiting for transfers between devices, group_work(): lax.psum_scatter(terms.reshape(rows, heads * width).astype(jnp.bfloat16),...  87.1 us
    all_gather x1, waiting for transfers between devices, group_work(): lax.all_gather(queries, 'inner', axis=0, tiled=True)  32.9 us
    ppermute x4, waiting for transfers between devices, passed_along(): return lax.ppermute(x, axis, [(i, (i + by) % count) for i in range(count)])  31.9 us
    all_gather x1, blocking collectives, group_work(): lax.all_gather(lse, 'inner', axis=0, tiled=True)  28.8 us
    all_gather x1, blocking collectives, group_work(): lax.all_gather(delta, 'inner', axis=0, tiled=True)  26.9 us
    ppermute x4, starting transfers between devices, passed_along(): return lax.ppermute(x, axis, [(i, (i + by) % count) for i in range(count)])  12.3 us
    dot_general x4, matrix products, head_block(): jnp.einsum('qhd,khd->hqk', ob, vb, preferred_element_type=jnp.float32)  9.28 us
  transfers between devices with their start and end apart: 7, of which 5 were waited for; matrix products, arithmetic and copies ran while one was open for 1% of the time, Pallas kernels for 0%

commit v1 on v0

v1 whole, which is shorter than its diff:
```python
import jax
import jax.numpy as jnp
from jax import lax
from jax.experimental import pallas as pl
from jax.experimental.pallas import tpu as pltpu
from jax.sharding import PartitionSpec as P

N_INNER = 8
WIDTH = 128
PAIR = 2 * WIDTH
STAT_ROWS = 16
LOG2E = 1.4426950408889634
SHIFTS = ((2, 0), (2, 1), (1, 0), (1, 1), (3, 0), (3, 1), (0, 1), (0, 0))


def moved_inner(i, shift, sign=1):
    dz, dc = shift
    return ((i // 2 + sign * dz) % 4) * 2 + (i + dc) % 2


def send_pairs(outer_count, shift, back):
    pairs = []
    for o in range(outer_count):
        for i in range(N_INNER):
            here = o * N_INNER + i
            there = ((o - 1) % outer_count) * N_INNER + moved_inner(i, shift)
            pairs.append((there, here) if back else (here, there))
    return pairs


def pack_kv(keys, values):
    rows = keys.shape[0]

    def kernel(k_ref, v_ref, out_ref, sem):
        copies = []
        for j in range(N_INNER):
            cols = pl.ds(j * PAIR, PAIR)
            copies.append(pltpu.make_async_copy(k_ref.at[:, cols], out_ref.at[j, pl.ds(0, rows)], sem.at[0, j]))
            copies.append(pltpu.make_async_copy(v_ref.at[:, cols], out_ref.at[j, pl.ds(rows, rows)], sem.at[1, j]))
        for c in copies:
            c.start()
        for c in copies:
            c.wait()

    return pl.pallas_call(
        kernel,
        out_shape=jax.ShapeDtypeStruct((N_INNER, 2 * rows, PAIR), keys.dtype),
        in_specs=[pl.BlockSpec(memory_space=pl.ANY)] * 2,
        out_specs=pl.BlockSpec(memory_space=pl.ANY),
        scratch_shapes=[pltpu.SemaphoreType.DMA((2, N_INNER))],
        name="pack_kv",
    )(keys, values)


def pack_q(chunk, queries, grad_out, stats):
    rows = queries.shape[0]

    def kernel(chunk_ref, q_ref, o_ref, s_ref, *rest):
        outs, sem = rest[:-1], rest[-1]
        copies = []
        for r, out in enumerate(outs):
            j = chunk_ref[r]
            cols = pl.ds(pl.multiple_of(j * PAIR, PAIR), PAIR)
            copies.append(pltpu.make_async_copy(q_ref.at[:, cols], out.at[pl.ds(0, rows)], sem.at[0, r]))
            copies.append(pltpu.make_async_copy(o_ref.at[:, cols], out.at[pl.ds(rows, rows)], sem.at[1, r]))
            copies.append(pltpu.make_async_copy(s_ref.at[j], out.at[pl.ds(2 * rows, STAT_ROWS)], sem.at[2, r]))
        for c in copies:
            c.start()
        for c in copies:
            c.wait()

    return pl.pallas_call(
        kernel,
        out_shape=[jax.ShapeDtypeStruct((2 * rows + STAT_ROWS, PAIR), queries.dtype)] * N_INNER,
        in_specs=[pl.BlockSpec(memory_space=pltpu.SMEM)] + [pl.BlockSpec(memory_space=pl.ANY)] * 3,
        out_specs=[pl.BlockSpec(memory_space=pl.ANY)] * N_INNER,
        scratch_shapes=[pltpu.SemaphoreType.DMA((3, N_INNER))],
        name="pack_q",
    )(chunk, queries, grad_out, stats)


def attend(kv, parts, kcol, qrow):
    rows = kv.shape[1] // 2
    half = rows // 2
    side = N_INNER * half
    scale = WIDTH ** -0.5
    tile = 256

    def kernel(kv_ref, kcol_ref, qrow_ref, *rest):
        ins, rest = rest[:N_INNER], rest[N_INNER:]
        dqs, rest = rest[:N_INNER], rest[N_INNER:]
        dkv_ref, q_s, o_s, k_s, v_s, l_s, d_s, dk_s, dv_s = rest
        for a in range(N_INNER):
            for part in range(2):
                to = pl.ds(part * side + a * half, half)
                at = part * half
                q_s[to, :] = ins[a][pl.ds(at, half), :]
                o_s[to, :] = ins[a][pl.ds(rows + at, half), :]
                k_s[to, :] = kv_ref[a, pl.ds(at, half), :]
                v_s[to, :] = kv_ref[a, pl.ds(rows + at, half), :]
            st = ins[a][pl.ds(2 * rows, STAT_ROWS), :].astype(jnp.float32)
            for h in range(2):
                for part in range(2):
                    lanes = slice(h * WIDTH + part * half, h * WIDTH + (part + 1) * half)
                    to = pl.ds(part * side + a * half, half)
                    l_s[pl.ds(h, 1), to] = st[0:1, lanes] * LOG2E
                    d_s[pl.ds(h, 1), to] = st[1:2, lanes]
        nt = (((1,), (1,)), ((), ()))
        f32 = jnp.float32
        for h in range(2):
            head = pl.ds(h * WIDTH, WIDTH)
            k_all = k_s[:, head]
            v_all = v_s[:, head]
            kt = k_all.astype(f32).T.astype(jnp.bfloat16)
            for step, (part, piece) in enumerate(((1, 0), (1, 1), (0, 0), (0, 1))):
                qs = pl.ds(part * side + piece * tile, tile)
                q = q_s[qs, head]
                o = o_s[qs, head]
                count = 2 * side if part else side
                l = l_s[pl.ds(h, 1), qs]
                d = d_s[pl.ds(h, 1), qs]
                s = lax.dot_general(k_all[:count], q, nt, preferred_element_type=f32)
                p = jnp.exp2(s * (scale * LOG2E) - l)
                qc = qrow_ref[:, pl.ds(piece * tile, tile)]
                if part:
                    p = jnp.concatenate([p[:side], jnp.where(kcol_ref[...] > qc, p[side:], 0.0)], 0)
                else:
                    p = jnp.where(kcol_ref[...] < qc, p, 0.0)
                dp = lax.dot_general(v_all[:count], o, nt, preferred_element_type=f32)
                ds = (p * (dp - d)).astype(jnp.bfloat16)
                dv = jnp.dot(p.astype(jnp.bfloat16), o, preferred_element_type=f32)
                dk = jnp.dot(ds, q, preferred_element_type=f32)
                dqt = jnp.dot(kt[:, :count], ds, preferred_element_type=f32)
                dq = (dqt * scale).T.astype(jnp.bfloat16)
                per = tile // half
                for a in range(per):
                    dqs[piece * per + a][pl.ds(part * half, half), head] = dq[a * half:(a + 1) * half]
                if step == 0:
                    dv_s[...] = dv
                    dk_s[...] = dk
                else:
                    dv_s[pl.ds(0, count), :] += dv
                    dk_s[pl.ds(0, count), :] += dk
            for b in range(N_INNER):
                for part in range(2):
                    at = pl.ds(part * side + b * half, half)
                    dkv_ref[b, pl.ds(part * half, half), head] = (dk_s[at, :] * scale).astype(jnp.bfloat16)
                    dkv_ref[b, pl.ds(rows + part * half, half), head] = dv_s[at, :].astype(jnp.bfloat16)

    vmem = pl.BlockSpec(memory_space=pltpu.VMEM)
    outs = pl.pallas_call(
        kernel,
        out_shape=[jax.ShapeDtypeStruct((rows, PAIR), jnp.bfloat16)] * N_INNER
        + [jax.ShapeDtypeStruct(kv.shape, jnp.bfloat16)],
        in_specs=[vmem] * (3 + N_INNER),
        out_specs=[vmem] * (N_INNER + 1),
        scratch_shapes=[pltpu.VMEM((2 * side, PAIR), jnp.bfloat16)] * 4
        + [pltpu.VMEM((2, 2 * side), jnp.float32)] * 2
        + [pltpu.VMEM((2 * side, WIDTH), jnp.float32)] * 2,
        compiler_params=pltpu.CompilerParams(vmem_limit_bytes=40 * 1024 * 1024),
        name="attend",
    )(kv, kcol, qrow, *parts)
    return outs[:N_INNER], outs[N_INNER]


def unpack_q(chunk, parts):
    rows = parts[0].shape[0]

    def kernel(chunk_ref, *rest):
        out = rest[-1]
        for r in range(N_INNER):
            cols = pl.ds(pl.multiple_of(chunk_ref[r] * PAIR, PAIR), PAIR)
            out[:, cols] = rest[r][...].astype(jnp.float32)

    vmem = pl.BlockSpec(memory_space=pltpu.VMEM)
    return pl.pallas_call(
        kernel,
        out_shape=jax.ShapeDtypeStruct((rows, N_INNER * PAIR), jnp.float32),
        in_specs=[pl.BlockSpec(memory_space=pltpu.SMEM)] + [vmem] * N_INNER,
        out_specs=vmem,
        name="unpack_q",
    )(chunk, *parts)


def unpack_kv(dkv):
    rows = dkv.shape[1] // 2

    def kernel(in_ref, dk_ref, dv_ref):
        dk_ref[...] = in_ref[0, pl.ds(0, rows), :].astype(jnp.float32)
        dv_ref[...] = in_ref[0, pl.ds(rows, rows), :].astype(jnp.float32)

    return pl.pallas_call(
        kernel,
        grid=(N_INNER,),
        out_shape=[jax.ShapeDtypeStruct((rows, N_INNER * PAIR), jnp.float32)] * 2,
        in_specs=[pl.BlockSpec((1, 2 * rows, PAIR), lambda j: (j, 0, 0))],
        out_specs=[pl.BlockSpec((rows, PAIR), lambda j: (0, j))] * 2,
        name="unpack_kv",
    )(dkv)


def shards(queries, keys, values, grad_out, lse, delta, span_table):
    outer_count = lax.axis_size("outer")
    outer_idx = lax.axis_index("outer")
    inner_idx = lax.axis_index("inner")
    rows = queries.shape[0]
    half = rows // 2
    chunk = jnp.stack([moved_inner(inner_idx, s) for s in SHIFTS]).astype(jnp.int32)
    senders = jnp.stack([moved_inner(inner_idx, s, -1) for s in SHIFTS]).astype(jnp.int32)

    kv = lax.all_to_all(pack_kv(keys, values), "inner", 0, 0, tiled=True)

    stats = jnp.stack([lse.T.reshape(N_INNER, PAIR), delta.T.reshape(N_INNER, PAIR)], axis=1)
    stats = jnp.pad(stats, ((0, 0), (0, STAT_ROWS - 2), (0, 0)))
    sent = pack_q(chunk, queries, grad_out, stats)
    axes = ("outer", "inner")
    parts = [lax.ppermute(x, axes, send_pairs(outer_count, s, False)) for x, s in zip(sent, SHIFTS)]

    first = span_table[:, 0].reshape(outer_count, N_INNER)
    key_c = lax.dynamic_index_in_dim(first, outer_idx, 0, keepdims=False)
    query_c = lax.dynamic_index_in_dim(first, (outer_idx + 1) % outer_count, 0, keepdims=False)[senders]
    kcol = jnp.repeat(key_c, half)[:, None]
    qrow = jnp.repeat(query_c, half)[None, :]

    dqs, dkv = attend(kv, parts, kcol, qrow)
    dkv = lax.all_to_all(dkv, "inner", 0, 0, tiled=True)
    back = [lax.ppermute(x, axes, send_pairs(outer_count, s, True)) for x, s in zip(dqs, SHIFTS)]
    grad_k, grad_v = unpack_kv(dkv)
    grad_q = unpack_q(chunk, back)
    return grad_q, grad_k, grad_v


def solution(mesh):
    placed = P(("outer", "inner"), None)
    return jax.shard_map(
        shards,
        mesh=mesh,
        in_specs=(placed,) * 6 + (P(),),
        out_specs=(placed,) * 3,
        check_vma=False,
    )
```

time: 411 us -> 281 us (0.68)
  the two profiles are of different devices: /device:TPU:64 before, /device:TPU:61 now
where the time goes in v1:
time: 281 us; the launch traced here: 280 us
  starting transfers between devices  123 us (44%)
  Pallas kernels  81.3 us (29%)
  waiting for transfers between devices  68.2 us (24%)
  local copies, waits for them, and re-layouts  5.63 us (2%)
    ppermute x8, starting transfers between devices, shards(): lax.ppermute(x, axes, send_pairs(outer_count, s, True))  60.2 us
    ppermute x8, starting transfers between devices, shards(): lax.ppermute(x, axes, send_pairs(outer_count, s, False))  39.7 us
    pallas_call x1, Pallas kernels, pack_q(): pl.pallas_call(kernel, out_shape=[jax.ShapeDtypeStruct((2 * rows + STAT_R...  35.7 us
    ppermute x8, waiting for transfers between devices, shards(): lax.ppermute(x, axes, send_pairs(outer_count, s, False))  35.1 us
    ppermute x8, waiting for transfers between devices, shards(): lax.ppermute(x, axes, send_pairs(outer_count, s, True))  33.1 us
    pallas_call x1, Pallas kernels, pack_kv(): pl.pallas_call(kernel, out_shape=jax.ShapeDtypeStruct((N_INNER, 2 * rows,...  33 us
    all_to_all x1, starting transfers between devices, shards(): kv = lax.all_to_all(pack_kv(keys, values), 'inner', 0, 0, tiled=True)  14.9 us
    all_to_all x1, starting transfers between devices, shards(): dkv = lax.all_to_all(dkv, 'inner', 0, 0, tiled=True)  8.55 us
  transfers between devices with their start and end apart: 18, of which 7 were waited for; matrix products, arithmetic and copies ran while one was open for 1% of the time, Pallas kernels for 14%

profile of v1, /device:TPU:61, one launch (start us, length us, event | category | flops | bytes accessed | tf_op | source)
XLA Modules:
  0.0 280.1 jit_solution(7025919731984191140)
XLA Ops:
  0.6 33.0 %pack_kv.1 = bf16[8,256,256]{2,1,0:T(8,128)(2,1)} custom-call(bf16[128,2048]{1,0:T(8,128)(2,1)} %k_ref.1, bf16[128,2048]{1,0:T(8,128)(2,1)} %v_ref.1), custom_call_target="tpu_custom_call" | custom-call | tf_op jit(solution)/shard_map/pack_kv/pallas_call | solution.py:45
  33.6 14.9 %all-to-all-start = ((bf16[8,256,256]{2,1,0:T(8,128)(2,1)}), bf16[8,256,256]{2,1,0:T(8,128)(2,1)S(1)}, u32[]{:S(2)}, u32[]{:S(2)}) async-start(bf16[8,256,256]{2,1,0:T(8,128)(2,1)} %pack_kv.1), calls=%async_computation | async-start | bytes 2097152 | tf_op jit(solution)/shard_map/all_to_all | solution.py:211
  48.5 0.7 copy-done.9
  49.2 0.7 copy-done.10
  49.9 0.7 stack.65.chunk_ref
  50.6 0.6 fusion.2.s_ref
  51.2 35.7 %pack_q.1 = (bf16[272,256]{1,0:T(8,128)(2,1)}, bf16[272,256]{1,0:T(8,128)(2,1)}, bf16[272,256]{1,0:T(8,128)(2,1)}, bf16[272,256]{1,0:T(8,128)(2,1)}, bf16[272,25...) custom-call(s32[8]{0:T(128)} %stack.65.chunk_ref, ...), custom_call_target="tpu_custom_call" | custom-call | tf_op jit(solution)/shard_map/pack_q/pallas_call | solution.py:72
  87.0 12.0 %collective-permute-start = (bf16[272,256]{1,0:T(8,128)(2,1)}, bf16[272,256]{1,0:T(8,128)(2,1)S(1)}, u32[]{:S(2)}, u32[]{:S(2)}) collective-permute-start(bf16[272,256]{1,0:T(8,128)(2,1)} %get-tuple-element.22), channel_id=1, source_target_pairs={{0,508},{1,509},{2,510},{3,511},{4,504},{5,505},{6,506},{7,507},{8... | collective-permute-start | bytes 417800 | tf_op jit(solution)/shard_map/ppermute | solution.py:217
  98.9 2.2 collective-permute-start.1
  101.1 9.9 %collective-permute-start.2 = (bf16[272,256]{1,0:T(8,128)(2,1)}, bf16[272,256]{1,0:T(8,128)(2,1)S(1)}, u32[]{:S(2)}, u32[]{:S(2)}) collective-permute-start(bf16[272,256]{1,0:T(8,128)(2,1)} %get-tuple-element.24), channel_id=1, source_target_pairs={{0,506},{1,507},{2,508},{3,509},{4,510},{5,511},{6,504},{7,505},{8... | collective-permute-start | bytes 417800 | tf_op jit(solution)/shard_map/ppermute | solution.py:217
  111.0 7.3 %collective-permute-start.3 = (bf16[272,256]{1,0:T(8,128)(2,1)}, bf16[272,256]{1,0:T(8,128)(2,1)S(1)}, u32[]{:S(2)}, u32[]{:S(2)}) collective-permute-start(bf16[272,256]{1,0:T(8,128)(2,1)} %get-tuple-element.25), channel_id=1, source_target_pairs={{0,507},{1,506},{2,509},{3,508},{4,511},{5,510},{6,505},{7,504},{8... | collective-permute-start | bytes 417800 | tf_op jit(solution)/shard_map/ppermute | solution.py:217
  118.3 2.2 collective-permute-start.4
  120.6 0.0 copy-start.11
  120.6 0.7 copy-done.11
  121.3 0.1 reshape_squeeze.3
  121.4 0.1 stack.74
  121.5 4.7 %collective-permute-done.rest_0_ = bf16[272,256]{1,0:T(8,128)(2,1)S(1)} collective-permute-done((bf16[272,256]{1,0:T(8,128)(2,1)}, bf16[272,256]{1,0:T(8,128)(2,1)S(1)}, u32[]{:S(2)}, u32[]{:S(2)}) %collective-permute-start) | collective-permute-done | bytes 139296 | tf_op jit(solution)/shard_map/ppermute | solution.py:217
  126.2 1.9 collective-permute-start.5
  128.1 3.4 %collective-permute-done.1.rest_1_ = bf16[272,256]{1,0:T(8,128)(2,1)S(1)} collective-permute-done((bf16[272,256]{1,0:T(8,128)(2,1)}, bf16[272,256]{1,0:T(8,128)(2,1)S(1)}, u32[]{:S(2)}, u32[]{:S(2)}) %collective-permute-start.1) | collective-permute-done | bytes 139296 | tf_op jit(solution)/shard_map/ppermute | solution.py:217
  131.5 2.4 collective-permute-start.6
  133.9 4.3 %collective-permute-done.2.rest_2_ = bf16[272,256]{1,0:T(8,128)(2,1)S(1)} collective-permute-done((bf16[272,256]{1,0:T(8,128)(2,1)}, bf16[272,256]{1,0:T(8,128)(2,1)S(1)}, u32[]{:S(2)}, u32[]{:S(2)}) %collective-permute-start.2) | collective-permute-done | bytes 139296 | tf_op jit(solution)/shard_map/ppermute | solution.py:217
  138.2 1.9 collective-permute-start.7
  140.1 0.6 gather_fusion
  140.8 0.1 broadcast_in_dim.8
  140.9 0.1 broadcast_in_dim_reshape.7.qrow_ref
  140.9 0.1 broadcast_in_dim.7
  141.0 0.2 broadcast_in_dim_reshape.8.kcol_ref
  141.2 0.0 collective-permute-done.3.rest_3_
  141.3 0.0 collective-permute-done.4.rest_4_
  141.3 12.0 %collective-permute-done.5.rest_5_ = bf16[272,256]{1,0:T(8,128)(2,1)S(1)} collective-permute-done((bf16[272,256]{1,0:T(8,128)(2,1)}, bf16[272,256]{1,0:T(8,128)(2,1)S(1)}, u32[]{:S(2)}, u32[]{:S(2)}) %collective-permute-start.5) | collective-permute-done | bytes 139296 | tf_op jit(solution)/shard_map/ppermute | solution.py:217
  153.2 10.7 %collective-permute-done.7.rest_7_ = bf16[272,256]{1,0:T(8,128)(2,1)S(1)} collective-permute-done((bf16[272,256]{1,0:T(8,128)(2,1)}, bf16[272,256]{1,0:T(8,128)(2,1)S(1)}, u32[]{:S(2)}, u32[]{:S(2)}) %collective-permute-start.7) | collective-permute-done | bytes 139296 | tf_op jit(solution)/shard_map/ppermute | solution.py:217
  163.9 5.1 %attend.1 = (bf16[128,256]{1,0:T(8,128)(2,1)S(1)}, bf16[128,256]{1,0:T(8,128)(2,1)S(1)}, bf16[128,256]{1,0:T(8,128)(2,1)S(1)}, bf16[128,256]{1,0:T(8,128)(2,1)S(...) custom-call(bf16[8,256,256]{2,1,0:T(8,128)(2,1)S(1)} %all-to-all-don, ...), custom_call_target="tpu_custom_call" | custom-call | tf_op jit(solution)/shard_map/attend/pallas_call | solution.py:151
  169.0 8.6 %all-to-all-start.1 = ((bf16[8,256,256]{2,1,0:T(8,128)(2,1)}), bf16[8,256,256]{2,1,0:T(8,128)(2,1)S(1)}, u32[]{:S(2)}, u32[]{:S(2)}) async-start(bf16[8,256,256]{2,1,0:T(8,128)(2,1)} %get-tuple-element.38), calls=%async_computation.1 | async-start | bytes 2097152 | tf_op jit(solution)/shard_map/all_to_all | solution.py:226
  177.5 13.6 %collective-permute-start.10 = (bf16[128,256]{1,0:T(8,128)(2,1)S(1)}, bf16[128,256]{1,0:T(8,128)(2,1)S(1)}, u32[]{:S(2)}, u32[]{:S(2)}) collective-permute-start(bf16[128,256]{1,0:T(8,128)(2,1)S(1)} %get-tuple-element.32), channel_id=1, source_target_pairs={{506,0},{507,1},{508,2},{509,3},{510,4},{511,5},{504,6},{505,7},{2... | collective-permute-start | bytes 196616 | tf_op jit(solution)/shard_map/ppermute | solution.py:227
  191.2 7.0 %collective-permute-start.11 = (bf16[128,256]{1,0:T(8,128)(2,1)S(1)}, bf16[128,256]{1,0:T(8,128)(2,1)S(1)}, u32[]{:S(2)}, u32[]{:S(2)}) collective-permute-start(bf16[128,256]{1,0:T(8,128)(2,1)S(1)} %get-tuple-element.33), channel_id=1, source_target_pairs={{507,0},{506,1},{509,2},{508,3},{511,4},{510,5},{505,6},{504,7},{3... | collective-permute-start | bytes 196616 | tf_op jit(solution)/shard_map/ppermute | solution.py:227
  198.2 1.9 collective-permute-start.12
  200.1 2.8 %collective-permute-start.13 = (bf16[128,256]{1,0:T(8,128)(2,1)S(1)}, bf16[128,256]{1,0:T(8,128)(2,1)S(1)}, u32[]{:S(2)}, u32[]{:S(2)}) collective-permute-start(bf16[128,256]{1,0:T(8,128)(2,1)S(1)} %get-tuple-element.35), channel_id=1, source_target_pairs={{511,0},{510,1},{505,2},{504,3},{507,4},{506,5},{509,6},{508,7},{7... | collective-permute-start | bytes 196616 | tf_op jit(solution)/shard_map/ppermute | solution.py:227
  203.0 1.9 collective-permute-start.14
  204.9 19.3 %collective-permute-done.10.rest_2_ = bf16[128,256]{1,0:T(8,128)(2,1)S(1)} collective-permute-done((bf16[128,256]{1,0:T(8,128)(2,1)S(1)}, bf16[128,256]{1,0:T(8,128)(2,1)S(1)}, u32[]{:S(2)}, u32[]{:S(2)}) %collective-permute-start.10) | collective-permute-done | bytes 65568 | tf_op jit(solution)/shard_map/ppermute | solution.py:227
  224.2 11.9 %collective-permute-start.15 = (bf16[128,256]{1,0:T(8,128)(2,1)S(1)}, bf16[128,256]{1,0:T(8,128)(2,1)S(1)}, u32[]{:S(2)}, u32[]{:S(2)}) collective-permute-start(bf16[128,256]{1,0:T(8,128)(2,1)S(1)} %get-tuple-element.37), channel_id=1, source_target_pairs={{504,0},{505,1},{506,2},{507,3},{508,4},{509,5},{510,6},{511,7},{0... | collective-permute-start | bytes 196616 | tf_op jit(solution)/shard_map/ppermute | solution.py:227
  236.1 17.5 %collective-permute-start.8 = (bf16[128,256]{1,0:T(8,128)(2,1)S(1)}, bf16[128,256]{1,0:T(8,128)(2,1)S(1)}, u32[]{:S(2)}, u32[]{:S(2)}) collective-permute-start(bf16[128,256]{1,0:T(8,128)(2,1)S(1)} %get-tuple-element.30), channel_id=1, source_target_pairs={{508,0},{509,1},{510,2},{511,3},{504,4},{505,5},{506,6},{507,7},{4... | collective-permute-start | bytes 196616 | tf_op jit(solution)/shard_map/ppermute | solution.py:227
  253.7 3.4 %collective-permute-start.9 = (bf16[128,256]{1,0:T(8,128)(2,1)S(1)}, bf16[128,256]{1,0:T(8,128)(2,1)S(1)}, u32[]{:S(2)}, u32[]{:S(2)}) collective-permute-start(bf16[128,256]{1,0:T(8,128)(2,1)S(1)} %get-tuple-element.31), channel_id=1, source_target_pairs={{509,0},{508,1},{511,2},{510,3},{505,4},{504,5},{507,6},{506,7},{5... | collective-permute-start | bytes 196616 | tf_op jit(solution)/shard_map/ppermute | solution.py:227
  257.2 0.0 copy-start.7
  257.2 13.8 %collective-permute-done.9.rest_1_ = bf16[128,256]{1,0:T(8,128)(2,1)S(1)} collective-permute-done((bf16[128,256]{1,0:T(8,128)(2,1)S(1)}, bf16[128,256]{1,0:T(8,128)(2,1)S(1)}, u32[]{:S(2)}, u32[]{:S(2)}) %collective-permute-start.9) | collective-permute-done | bytes 65568 | tf_op jit(solution)/shard_map/ppermute | solution.py:227
  271.0 0.6 copy-done.8
  271.7 2.1 unpack_q.1
  273.8 1.0 copy-done
  274.7 5.4 %unpack_kv.1 = (f32[128,2048]{1,0:T(8,128)}, f32[128,2048]{1,0:T(8,128)}) custom-call(bf16[8,256,256]{2,1,0:T(8,128)(2,1)} %copy-done), custom_call_target="tpu_custom_call" | custom-call | tf_op jit(solution)/shard_map/unpack_kv/pallas_call | solution.py:192
  (32 shorter events, 0.1 us)
Async XLA Ops:
  33.6 130.3 %all-to-all-start = ((bf16[8,256,256]{2,1,0:T(8,128)(2,1)}), bf16[8,256,256]{2,1,0:T(8,128)(2,1)S(1)}, u32[]{:S(2)}, u32[]{:S(2)}) async-start(bf16[8,256,256]{2,1,0:T(8,128)(2,1)} %pack_kv.1), calls=%async_computation | async-start | bytes 2097152 | tf_op jit(solution)/shard_map/all_to_all | solution.py:211
  48.5 0.7 copy-start.9
  49.2 0.7 copy-start.10
  87.0 39.3 %collective-permute-start = (bf16[272,256]{1,0:T(8,128)(2,1)}, bf16[272,256]{1,0:T(8,128)(2,1)S(1)}, u32[]{:S(2)}, u32[]{:S(2)}) collective-permute-start(bf16[272,256]{1,0:T(8,128)(2,1)} %get-tuple-element.22), channel_id=1, source_target_pairs={{0,508},{1,509},{2,510},{3,511},{4,504},{5,505},{6,506},{7,507},{8... | collective-permute-start | bytes 417800 | tf_op jit(solution)/shard_map/ppermute | solution.py:217
  98.9 32.6 %collective-permute-start.1 = (bf16[272,256]{1,0:T(8,128)(2,1)}, bf16[272,256]{1,0:T(8,128)(2,1)S(1)}, u32[]{:S(2)}, u32[]{:S(2)}) collective-permute-start(bf16[272,256]{1,0:T(8,128)(2,1)} %get-tuple-element.23), channel_id=1, source_target_pairs={{0,509},{1,508},{2,511},{3,510},{4,505},{5,504},{6,507},{7,506},{8... | collective-permute-start | bytes 417800 | tf_op jit(solution)/shard_map/ppermute | solution.py:217
  101.1 37.1 %collective-permute-start.2 = (bf16[272,256]{1,0:T(8,128)(2,1)}, bf16[272,256]{1,0:T(8,128)(2,1)S(1)}, u32[]{:S(2)}, u32[]{:S(2)}) collective-permute-start(bf16[272,256]{1,0:T(8,128)(2,1)} %get-tuple-element.24), channel_id=1, source_target_pairs={{0,506},{1,507},{2,508},{3,509},{4,510},{5,511},{6,504},{7,505},{8... | collective-permute-start | bytes 417800 | tf_op jit(solution)/shard_map/ppermute | solution.py:217
  111.0 30.2 %collective-permute-start.3 = (bf16[272,256]{1,0:T(8,128)(2,1)}, bf16[272,256]{1,0:T(8,128)(2,1)S(1)}, u32[]{:S(2)}, u32[]{:S(2)}) collective-permute-start(bf16[272,256]{1,0:T(8,128)(2,1)} %get-tuple-element.25), channel_id=1, source_target_pairs={{0,507},{1,506},{2,509},{3,508},{4,511},{5,510},{6,505},{7,504},{8... | collective-permute-start | bytes 417800 | tf_op jit(solution)/shard_map/ppermute | solution.py:217
  118.3 22.9 %collective-permute-start.4 = (bf16[272,256]{1,0:T(8,128)(2,1)}, bf16[272,256]{1,0:T(8,128)(2,1)S(1)}, u32[]{:S(2)}, u32[]{:S(2)}) collective-permute-start(bf16[272,256]{1,0:T(8,128)(2,1)} %get-tuple-element.26), channel_id=1, source_target_pairs={{0,510},{1,511},{2,504},{3,505},{4,506},{5,507},{6,508},{7,509},{8... | collective-permute-start | bytes 417800 | tf_op jit(solution)/shard_map/ppermute | solution.py:217
  120.6 0.7 copy-start.11
  126.2 27.0 %collective-permute-start.5 = (bf16[272,256]{1,0:T(8,128)(2,1)}, bf16[272,256]{1,0:T(8,128)(2,1)S(1)}, u32[]{:S(2)}, u32[]{:S(2)}) collective-permute-start(bf16[272,256]{1,0:T(8,128)(2,1)} %get-tuple-element.27), channel_id=1, source_target_pairs={{0,511},{1,510},{2,505},{3,504},{4,507},{5,506},{6,509},{7,508},{8... | collective-permute-start | bytes 417800 | tf_op jit(solution)/shard_map/ppermute | solution.py:217
  131.5 21.7 %collective-permute-start.6 = (bf16[272,256]{1,0:T(8,128)(2,1)}, bf16[272,256]{1,0:T(8,128)(2,1)S(1)}, u32[]{:S(2)}, u32[]{:S(2)}) collective-permute-start(bf16[272,256]{1,0:T(8,128)(2,1)} %get-tuple-element.28), channel_id=1, source_target_pairs={{0,505},{1,504},{2,507},{3,506},{4,509},{5,508},{6,511},{7,510},{8... | collective-permute-start | bytes 417800 | tf_op jit(solution)/shard_map/ppermute | solution.py:217
  138.2 25.7 %collective-permute-start.7 = (bf16[272,256]{1,0:T(8,128)(2,1)}, bf16[272,256]{1,0:T(8,128)(2,1)S(1)}, u32[]{:S(2)}, u32[]{:S(2)}) collective-permute-start(bf16[272,256]{1,0:T(8,128)(2,1)} %get-tuple-element.29), channel_id=1, source_target_pairs={{0,504},{1,505},{2,506},{3,507},{4,508},{5,509},{6,510},{7,511},{8... | collective-permute-start | bytes 417800 | tf_op jit(solution)/shard_map/ppermute | solution.py:217
  169.0 104.8 %all-to-all-start.1 = ((bf16[8,256,256]{2,1,0:T(8,128)(2,1)}), bf16[8,256,256]{2,1,0:T(8,128)(2,1)S(1)}, u32[]{:S(2)}, u32[]{:S(2)}) async-start(bf16[8,256,256]{2,1,0:T(8,128)(2,1)} %get-tuple-element.38), calls=%async_computation.1 | async-start | bytes 2097152 | tf_op jit(solution)/shard_map/all_to_all | solution.py:226
  177.5 46.6 %collective-permute-start.10 = (bf16[128,256]{1,0:T(8,128)(2,1)S(1)}, bf16[128,256]{1,0:T(8,128)(2,1)S(1)}, u32[]{:S(2)}, u32[]{:S(2)}) collective-permute-start(bf16[128,256]{1,0:T(8,128)(2,1)S(1)} %get-tuple-element.32), channel_id=1, source_target_pairs={{506,0},{507,1},{508,2},{509,3},{510,4},{511,5},{504,6},{505,7},{2... | collective-permute-start | bytes 196616 | tf_op jit(solution)/shard_map/ppermute | solution.py:227
  191.2 44.9 %collective-permute-start.11 = (bf16[128,256]{1,0:T(8,128)(2,1)S(1)}, bf16[128,256]{1,0:T(8,128)(2,1)S(1)}, u32[]{:S(2)}, u32[]{:S(2)}) collective-permute-start(bf16[128,256]{1,0:T(8,128)(2,1)S(1)} %get-tuple-element.33), channel_id=1, source_target_pairs={{507,0},{506,1},{509,2},{508,3},{511,4},{510,5},{505,6},{504,7},{3... | collective-permute-start | bytes 196616 | tf_op jit(solution)/shard_map/ppermute | solution.py:227
  198.2 55.5 %collective-permute-start.12 = (bf16[128,256]{1,0:T(8,128)(2,1)S(1)}, bf16[128,256]{1,0:T(8,128)(2,1)S(1)}, u32[]{:S(2)}, u32[]{:S(2)}) collective-permute-start(bf16[128,256]{1,0:T(8,128)(2,1)S(1)} %get-tuple-element.34), channel_id=1, source_target_pairs={{510,0},{511,1},{504,2},{505,3},{506,4},{507,5},{508,6},{509,7},{6... | collective-permute-start | bytes 196616 | tf_op jit(solution)/shard_map/ppermute | solution.py:227
  200.1 57.0 %collective-permute-start.13 = (bf16[128,256]{1,0:T(8,128)(2,1)S(1)}, bf16[128,256]{1,0:T(8,128)(2,1)S(1)}, u32[]{:S(2)}, u32[]{:S(2)}) collective-permute-start(bf16[128,256]{1,0:T(8,128)(2,1)S(1)} %get-tuple-element.35), channel_id=1, source_target_pairs={{511,0},{510,1},{505,2},{504,3},{507,4},{506,5},{509,6},{508,7},{7... | collective-permute-start | bytes 196616 | tf_op jit(solution)/shard_map/ppermute | solution.py:227
  203.0 54.2 %collective-permute-start.14 = (bf16[128,256]{1,0:T(8,128)(2,1)S(1)}, bf16[128,256]{1,0:T(8,128)(2,1)S(1)}, u32[]{:S(2)}, u32[]{:S(2)}) collective-permute-start(bf16[128,256]{1,0:T(8,128)(2,1)S(1)} %get-tuple-element.36), channel_id=1, source_target_pairs={{505,0},{504,1},{507,2},{506,3},{509,4},{508,5},{511,6},{510,7},{1... | collective-permute-start | bytes 196616 | tf_op jit(solution)/shard_map/ppermute | solution.py:227
  224.2 46.8 %copy-start.1 = (bf16[128,256]{1,0:T(8,128)(2,1)}, bf16[128,256]{1,0:T(8,128)(2,1)S(1)}, u32[]{:S(2)}) copy-start(bf16[128,256]{1,0:T(8,128)(2,1)S(1)} %collective-permute-done.10.rest_2_) | copy-start | bytes 196612
  224.2 33.0 %collective-permute-start.15 = (bf16[128,256]{1,0:T(8,128)(2,1)S(1)}, bf16[128,256]{1,0:T(8,128)(2,1)S(1)}, u32[]{:S(2)}, u32[]{:S(2)}) collective-permute-start(bf16[128,256]{1,0:T(8,128)(2,1)S(1)} %get-tuple-element.37), channel_id=1, source_target_pairs={{504,0},{505,1},{506,2},{507,3},{508,4},{509,5},{510,6},{511,7},{0... | collective-permute-start | bytes 196616 | tf_op jit(solution)/shard_map/ppermute | solution.py:227
  236.1 34.9 %copy-start.2 = (bf16[128,256]{1,0:T(8,128)(2,1)}, bf16[128,256]{1,0:T(8,128)(2,1)S(1)}, u32[]{:S(2)}) copy-start(bf16[128,256]{1,0:T(8,128)(2,1)S(1)} %collective-permute-done.11.rest_3_) | copy-start | bytes 196612
  236.1 21.1 %collective-permute-start.8 = (bf16[128,256]{1,0:T(8,128)(2,1)S(1)}, bf16[128,256]{1,0:T(8,128)(2,1)S(1)}, u32[]{:S(2)}, u32[]{:S(2)}) collective-permute-start(bf16[128,256]{1,0:T(8,128)(2,1)S(1)} %get-tuple-element.30), channel_id=1, source_target_pairs={{508,0},{509,1},{510,2},{511,3},{504,4},{505,5},{506,6},{507,7},{4... | collective-permute-start | bytes 196616 | tf_op jit(solution)/shard_map/ppermute | solution.py:227
  253.7 17.3 %copy-start.3 = (bf16[128,256]{1,0:T(8,128)(2,1)}, bf16[128,256]{1,0:T(8,128)(2,1)S(1)}, u32[]{:S(2)}) copy-start(bf16[128,256]{1,0:T(8,128)(2,1)S(1)} %collective-permute-done.12.rest_4_) | copy-start | bytes 196612
  253.7 17.3 %collective-permute-start.9 = (bf16[128,256]{1,0:T(8,128)(2,1)S(1)}, bf16[128,256]{1,0:T(8,128)(2,1)S(1)}, u32[]{:S(2)}, u32[]{:S(2)}) collective-permute-start(bf16[128,256]{1,0:T(8,128)(2,1)S(1)} %get-tuple-element.31), channel_id=1, source_target_pairs={{509,0},{508,1},{511,2},{510,3},{505,4},{504,5},{507,6},{506,7},{5... | collective-permute-start | bytes 196616 | tf_op jit(solution)/shard_map/ppermute | solution.py:227
  257.2 13.8 %copy-start.4 = (bf16[128,256]{1,0:T(8,128)(2,1)}, bf16[128,256]{1,0:T(8,128)(2,1)S(1)}, u32[]{:S(2)}) copy-start(bf16[128,256]{1,0:T(8,128)(2,1)S(1)} %collective-permute-done.13.rest_5_) | copy-start | bytes 196612
  257.2 13.8 %copy-start.5 = (bf16[128,256]{1,0:T(8,128)(2,1)}, bf16[128,256]{1,0:T(8,128)(2,1)S(1)}, u32[]{:S(2)}) copy-start(bf16[128,256]{1,0:T(8,128)(2,1)S(1)} %collective-permute-done.14.rest_6_) | copy-start | bytes 196612
  257.2 13.8 %copy-start.6 = (bf16[128,256]{1,0:T(8,128)(2,1)}, bf16[128,256]{1,0:T(8,128)(2,1)S(1)}, u32[]{:S(2)}) copy-start(bf16[128,256]{1,0:T(8,128)(2,1)S(1)} %collective-permute-done.15.rest_7_) | copy-start | bytes 196612
  257.2 13.8 %copy-start.7 = (bf16[128,256]{1,0:T(8,128)(2,1)}, bf16[128,256]{1,0:T(8,128)(2,1)S(1)}, u32[]{:S(2)}) copy-start(bf16[128,256]{1,0:T(8,128)(2,1)S(1)} %collective-permute-done.8.rest_0_) | copy-start | bytes 196612
  271.0 0.6 copy-start.8
  273.8 1.0 copy-start

commit v2 on v1

v2 whole, which is shorter than its diff:
```python
import jax
import jax.numpy as jnp
from jax import lax
from jax.experimental import pallas as pl
from jax.experimental.pallas import tpu as pltpu
from jax.sharding import PartitionSpec as P

N_INNER = 8
WIDTH = 128
PAIR = 2 * WIDTH
STAT_ROWS = 16
LOG2E = 1.4426950408889634
CHIPS = 4


def moved_inner(i, dz, dc, sign=1):
    return ((i // 2 + sign * dz) % 4) * 2 + (i + dc) % 2


def send_pairs(outer_count, dz, back):
    pairs = []
    for o in range(outer_count):
        for i in range(N_INNER):
            here = o * N_INNER + i
            there = ((o - 1) % outer_count) * N_INNER + moved_inner(i, dz, 0)
            pairs.append((there, here) if back else (here, there))
    return pairs


def to_sibling(x):
    return lax.ppermute(x, "inner", [(i, i ^ 1) for i in range(N_INNER)])


VMEM = pl.BlockSpec(memory_space=pltpu.VMEM)
SMEM = pl.BlockSpec(memory_space=pltpu.SMEM)


def pack_kv(keys, values):
    rows = keys.shape[0]

    def kernel(k_ref, v_ref, out_ref):
        for j in range(N_INNER):
            cols = pl.ds(j * PAIR, PAIR)
            out_ref[j, pl.ds(0, rows), :] = k_ref[:, cols]
            out_ref[j, pl.ds(rows, rows), :] = v_ref[:, cols]

    return pl.pallas_call(
        kernel,
        out_shape=jax.ShapeDtypeStruct((N_INNER, 2 * rows, PAIR), keys.dtype),
        in_specs=[VMEM] * 2,
        out_specs=VMEM,
        name="pack_kv",
    )(keys, values)


def chunk_of(q_ref, o_ref, s_ref, j, out, at):
    rows = q_ref.shape[0]
    cols = pl.ds(pl.multiple_of(j * PAIR, PAIR), PAIR)
    out[at + (pl.ds(0, rows), slice(None))] = q_ref[:, cols]
    out[at + (pl.ds(rows, rows), slice(None))] = o_ref[:, cols]
    out[at + (pl.ds(2 * rows, STAT_ROWS), slice(None))] = s_ref[j]


def pack_for_sibling(chunk, queries, grad_out, stats):
    rows = queries.shape[0]

    def kernel(chunk_ref, q_ref, o_ref, s_ref, out_ref):
        for dz in range(CHIPS):
            chunk_of(q_ref, o_ref, s_ref, chunk_ref[2 * dz + 1], out_ref, (dz,))

    return pl.pallas_call(
        kernel,
        out_shape=jax.ShapeDtypeStruct((CHIPS, 2 * rows + STAT_ROWS, PAIR), queries.dtype),
        in_specs=[SMEM] + [VMEM] * 3,
        out_specs=VMEM,
        name="pack_for_sibling",
    )(chunk, queries, grad_out, stats)


def pack_q(chunk, queries, grad_out, stats, from_sibling):
    rows = queries.shape[0]

    def kernel(chunk_ref, q_ref, o_ref, s_ref, x_ref, *outs):
        for dz, out in enumerate(outs):
            chunk_of(q_ref, o_ref, s_ref, chunk_ref[2 * dz], out, (0,))
            out[1] = x_ref[dz]

    return pl.pallas_call(
        kernel,
        out_shape=[jax.ShapeDtypeStruct((2, 2 * rows + STAT_ROWS, PAIR), queries.dtype)] * CHIPS,
        in_specs=[SMEM] + [VMEM] * 4,
        out_specs=[VMEM] * CHIPS,
        name="pack_q",
    )(chunk, queries, grad_out, stats, from_sibling)


def pack_dq(own, from_sibling):
    def kernel(own_ref, x_ref, *outs):
        for dz, out in enumerate(outs):
            out[0] = own_ref[dz]
            out[1] = x_ref[dz]

    return pl.pallas_call(
        kernel,
        out_shape=[jax.ShapeDtypeStruct((2,) + own.shape[1:], own.dtype)] * CHIPS,
        in_specs=[VMEM] * 2,
        out_specs=[VMEM] * CHIPS,
        name="pack_dq",
    )(own, from_sibling)


def attend(kv, parts, kcol, qrow):
    rows = kv.shape[1] // 2
    half = rows // 2
    side = N_INNER * half
    scale = WIDTH ** -0.5
    tile = 256

    def kernel(kv_ref, kcol_ref, qrow_ref, *rest):
        ins, rest = rest[:CHIPS], rest[CHIPS:]
        ins = [ins[a // 2].at[a % 2] for a in range(N_INNER)]
        dqs = [rest[a % 2].at[a // 2] for a in range(N_INNER)]
        dkv_ref, q_s, o_s, k_s, v_s, l_s, d_s, dk_s, dv_s = rest[2:]
        for a in range(N_INNER):
            for part in range(2):
                to = pl.ds(part * side + a * half, half)
                at = part * half
                q_s[to, :] = ins[a][pl.ds(at, half), :]
                o_s[to, :] = ins[a][pl.ds(rows + at, half), :]
                k_s[to, :] = kv_ref[a, pl.ds(at, half), :]
                v_s[to, :] = kv_ref[a, pl.ds(rows + at, half), :]
            st = ins[a][pl.ds(2 * rows, STAT_ROWS), :].astype(jnp.float32)
            for h in range(2):
                for part in range(2):
                    lanes = slice(h * WIDTH + part * half, h * WIDTH + (part + 1) * half)
                    to = pl.ds(part * side + a * half, half)
                    l_s[pl.ds(h, 1), to] = st[0:1, lanes] * LOG2E
                    d_s[pl.ds(h, 1), to] = st[1:2, lanes]
        nt = (((1,), (1,)), ((), ()))
        f32 = jnp.float32
        for h in range(2):
            head = pl.ds(h * WIDTH, WIDTH)
            k_all = k_s[:, head]
            v_all = v_s[:, head]
            kt = k_all.astype(f32).T.astype(jnp.bfloat16)
            for step, (part, piece) in enumerate(((1, 0), (1, 1), (0, 0), (0, 1))):
                qs = pl.ds(part * side + piece * tile, tile)
                q = q_s[qs, head]
                o = o_s[qs, head]
                count = 2 * side if part else side
                l = l_s[pl.ds(h, 1), qs]
                d = d_s[pl.ds(h, 1), qs]
                s = lax.dot_general(k_all[:count], q, nt, preferred_element_type=f32)
                p = jnp.exp2(s * (scale * LOG2E) - l)
                qc = qrow_ref[:, pl.ds(piece * tile, tile)]
                if part:
                    p = jnp.concatenate([p[:side], jnp.where(kcol_ref[...] > qc, p[side:], 0.0)], 0)
                else:
                    p = jnp.where(kcol_ref[...] < qc, p, 0.0)
                dp = lax.dot_general(v_all[:count], o, nt, preferred_element_type=f32)
                ds = (p * (dp - d)).astype(jnp.bfloat16)
                dv = jnp.dot(p.astype(jnp.bfloat16), o, preferred_element_type=f32)
                dk = jnp.dot(ds, q, preferred_element_type=f32)
                dqt = jnp.dot(kt[:, :count], ds, preferred_element_type=f32)
                dq = (dqt * scale).T.astype(jnp.bfloat16)
                per = tile // half
                for a in range(per):
                    dqs[piece * per + a][pl.ds(part * half, half), head] = dq[a * half:(a + 1) * half]
                if step == 0:
                    dv_s[...] = dv
                    dk_s[...] = dk
                else:
                    dv_s[pl.ds(0, count), :] += dv
                    dk_s[pl.ds(0, count), :] += dk
            for b in range(N_INNER):
                for part in range(2):
                    at = pl.ds(part * side + b * half, half)
                    dkv_ref[b, pl.ds(part * half, half), head] = (dk_s[at, :] * scale).astype(jnp.bfloat16)
                    dkv_ref[b, pl.ds(rows + part * half, half), head] = dv_s[at, :].astype(jnp.bfloat16)

    return pl.pallas_call(
        kernel,
        out_shape=[jax.ShapeDtypeStruct((CHIPS, rows, PAIR), jnp.bfloat16)] * 2
        + [jax.ShapeDtypeStruct(kv.shape, jnp.bfloat16)],
        in_specs=[VMEM] * (3 + CHIPS),
        out_specs=[VMEM] * 3,
        scratch_shapes=[pltpu.VMEM((2 * side, PAIR), jnp.bfloat16)] * 4
        + [pltpu.VMEM((2, 2 * side), jnp.float32)] * 2
        + [pltpu.VMEM((2 * side, WIDTH), jnp.float32)] * 2,
        compiler_params=pltpu.CompilerParams(vmem_limit_bytes=40 * 1024 * 1024),
        name="attend",
    )(kv, kcol, qrow, *parts)


def unpack_q(chunk, parts):
    rows = parts[0].shape[1]

    def kernel(chunk_ref, *rest):
        out = rest[-1]
        for r in range(N_INNER):
            cols = pl.ds(pl.multiple_of(chunk_ref[r] * PAIR, PAIR), PAIR)
            out[:, cols] = rest[r // 2][r % 2].astype(jnp.float32)

    return pl.pallas_call(
        kernel,
        out_shape=jax.ShapeDtypeStruct((rows, N_INNER * PAIR), jnp.float32),
        in_specs=[SMEM] + [VMEM] * CHIPS,
        out_specs=VMEM,
        name="unpack_q",
    )(chunk, *parts)


def unpack_kv(dkv):
    rows = dkv.shape[1] // 2

    def kernel(in_ref, dk_ref, dv_ref):
        for j in range(N_INNER):
            cols = pl.ds(j * PAIR, PAIR)
            dk_ref[:, cols] = in_ref[j, pl.ds(0, rows), :].astype(jnp.float32)
            dv_ref[:, cols] = in_ref[j, pl.ds(rows, rows), :].astype(jnp.float32)

    return pl.pallas_call(
        kernel,
        out_shape=[jax.ShapeDtypeStruct((rows, N_INNER * PAIR), jnp.float32)] * 2,
        in_specs=[VMEM],
        out_specs=[VMEM] * 2,
        name="unpack_kv",
    )(dkv)


def shards(queries, keys, values, grad_out, lse, delta, span_table):
    outer_count = lax.axis_size("outer")
    outer_idx = lax.axis_index("outer")
    inner_idx = lax.axis_index("inner")
    rows = queries.shape[0]
    half = rows // 2
    turns = [(dz, dc) for dz in range(CHIPS) for dc in range(2)]
    chunk = jnp.stack([moved_inner(inner_idx, *t) for t in turns]).astype(jnp.int32)
    senders = jnp.stack([moved_inner(inner_idx, *t, -1) for t in turns]).astype(jnp.int32)

    kv = lax.all_to_all(pack_kv(keys, values), "inner", 0, 0, tiled=True)

    stats = jnp.stack([lse.T.reshape(N_INNER, PAIR), delta.T.reshape(N_INNER, PAIR)], axis=1)
    stats = jnp.pad(stats, ((0, 0), (0, STAT_ROWS - 2), (0, 0)))
    crossed = to_sibling(pack_for_sibling(chunk, queries, grad_out, stats))
    sent = pack_q(chunk, queries, grad_out, stats, crossed)
    axes = ("outer", "inner")
    parts = [lax.ppermute(x, axes, send_pairs(outer_count, dz, False)) for dz, x in enumerate(sent)]

    first = span_table[:, 0].reshape(outer_count, N_INNER)
    key_c = lax.dynamic_index_in_dim(first, outer_idx, 0, keepdims=False)
    query_c = lax.dynamic_index_in_dim(first, (outer_idx + 1) % outer_count, 0, keepdims=False)[senders]
    kcol = jnp.repeat(key_c, half)[:, None]
    qrow = jnp.repeat(query_c, half)[None, :]

    own_dq, sibling_dq, dkv = attend(kv, parts, kcol, qrow)
    dkv = lax.all_to_all(dkv, "inner", 0, 0, tiled=True)
    sent = pack_dq(own_dq, to_sibling(sibling_dq))
    back = [lax.ppermute(x, axes, send_pairs(outer_count, dz, True)) for dz, x in enumerate(sent)]
    grad_k, grad_v = unpack_kv(dkv)
    grad_q = unpack_q(chunk, back)
    return grad_q, grad_k, grad_v


def solution(mesh):
    placed = P(("outer", "inner"), None)
    return jax.shard_map(
        shards,
        mesh=mesh,
        in_specs=(placed,) * 6 + (P(),),
        out_specs=(placed,) * 3,
        check_vma=False,
    )
```

time: 281 us -> 237 us (0.84)
  the two profiles are of different devices: /device:TPU:61 before, /device:TPU:97 now
where the time goes in v2:
time: 237 us; the launch traced here: 236 us
  waiting for transfers between devices  129 us (54%)
  starting transfers between devices  78.8 us (33%)
  Pallas kernels  18.6 us (8%)
  local copies, waits for them, and re-layouts  7.78 us (3%)
    ppermute x4, waiting for transfers between devices, shards(): lax.ppermute(x, axes, send_pairs(outer_count, dz, True))  66.1 us
    ppermute x4, waiting for transfers between devices, shards(): lax.ppermute(x, axes, send_pairs(outer_count, dz, False))  59.7 us
    ppermute x4, starting transfers between devices, shards(): lax.ppermute(x, axes, send_pairs(outer_count, dz, False))  28.8 us
    all_to_all x1, starting transfers between devices, shards(): dkv = lax.all_to_all(dkv, 'inner', 0, 0, tiled=True)  16.6 us
    ppermute x4, starting transfers between devices, shards(): lax.ppermute(x, axes, send_pairs(outer_count, dz, True))  16.5 us
    all_to_all x1, starting transfers between devices, shards(): kv = lax.all_to_all(pack_kv(keys, values), 'inner', 0, 0, tiled=True)  13.1 us
    unnamed x22, local copies, waits for them, and re-layouts  5.86 us
    pallas_call x1, Pallas kernels, attend(): pl.pallas_call(kernel, out_shape=[jax.ShapeDtypeStruct((CHIPS, rows, PAIR...  5.1 us
  transfers between devices with their start and end apart: 12, of which 8 were waited for; matrix products, arithmetic and copies ran while one was open for 1% of the time, Pallas kernels for 4%

profile of v2, /device:TPU:97, one launch (start us, length us, event | category | flops | bytes accessed | tf_op | source)
XLA Modules:
  0.0 235.8 jit_solution(1551400252052895028)
XLA Ops:
  0.6 2.2 pack_kv.1
  2.9 13.1 %all-to-all-start = ((bf16[8,256,256]{2,1,0:T(8,128)(2,1)}), bf16[8,256,256]{2,1,0:T(8,128)(2,1)S(1)}, u32[]{:S(2)}, u32[]{:S(2)}) async-start(bf16[8,256,256]{2,1,0:T(8,128)(2,1)} %pack_kv.1), calls=%async_computation | async-start | bytes 2097152 | tf_op jit(solution)/shard_map/all_to_all | solution.py:241
  15.9 0.7 copy-done.8
  16.6 0.7 copy-done.9
  17.3 0.6 stack.65.chunk_ref
  17.9 0.6 fusion.2.s_ref
  18.6 2.1 pack_for_sibling.1
  20.7 1.9 collective-permute-start
  22.6 0.1 stack.74
  22.8 2.0 collective-permute-done.x_ref
  24.7 0.8 copy-done.2
  25.5 2.5 %pack_q.1 = (bf16[2,272,256]{2,1,0:T(8,128)(2,1)}, bf16[2,272,256]{2,1,0:T(8,128)(2,1)}, bf16[2,272,256]{2,1,0:T(8,128)(2,1)}, bf16[2,272,256]{2,1,0:T(8,128)(2,1)}) custom-call(s32[8]{0:T(128)} %stack.65.chunk_ref, bf16[128,2048]{1,0:T(8,128)(2,1)} %q_ref.3, bf16[128,2048]{1,0:T(8,128)(2,1)} %o_ref.3, bf16[8,16,256]{2,1,0:T(8,128)(2,1)} %fusion.2.s_ref, ...), custom_call_target="tpu_custom_call" | custom-call | tf_op jit(solution)/shard_map/pack_q/pallas_call | solution.py:88
  28.0 7.4 %collective-permute-start.1 = (bf16[2,272,256]{2,1,0:T(8,128)(2,1)}, bf16[2,272,256]{2,1,0:T(8,128)(2,1)S(1)}, u32[]{:S(2)}, u32[]{:S(2)}) collective-permute-start(bf16[2,272,256]{2,1,0:T(8,128)(2,1)} %get-tuple-element.16), channel_id=1, source_target_pairs={{0,504},{1,505},{2,506},{3,507},{4,508},{5,509},{6,510},{7,511},{8... | collective-permute-start | bytes 835592 | tf_op jit(solution)/shard_map/ppermute | solution.py:248
  35.4 6.6 %collective-permute-start.2 = (bf16[2,272,256]{2,1,0:T(8,128)(2,1)}, bf16[2,272,256]{2,1,0:T(8,128)(2,1)S(1)}, u32[]{:S(2)}, u32[]{:S(2)}) collective-permute-start(bf16[2,272,256]{2,1,0:T(8,128)(2,1)} %get-tuple-element.17), channel_id=1, source_target_pairs={{0,506},{1,507},{2,508},{3,509},{4,510},{5,511},{6,504},{7,505},{8... | collective-permute-start | bytes 835592 | tf_op jit(solution)/shard_map/ppermute | solution.py:248
  42.0 7.0 %collective-permute-start.3 = (bf16[2,272,256]{2,1,0:T(8,128)(2,1)}, bf16[2,272,256]{2,1,0:T(8,128)(2,1)S(1)}, u32[]{:S(2)}, u32[]{:S(2)}) collective-permute-start(bf16[2,272,256]{2,1,0:T(8,128)(2,1)} %get-tuple-element.18), channel_id=1, source_target_pairs={{0,508},{1,509},{2,510},{3,511},{4,504},{5,505},{6,506},{7,507},{8... | collective-permute-start | bytes 835592 | tf_op jit(solution)/shard_map/ppermute | solution.py:248
  48.9 7.9 %collective-permute-start.4 = (bf16[2,272,256]{2,1,0:T(8,128)(2,1)}, bf16[2,272,256]{2,1,0:T(8,128)(2,1)S(1)}, u32[]{:S(2)}, u32[]{:S(2)}) collective-permute-start(bf16[2,272,256]{2,1,0:T(8,128)(2,1)} %get-tuple-element.19), channel_id=1, source_target_pairs={{0,510},{1,511},{2,504},{3,505},{4,506},{5,507},{6,508},{7,509},{8... | collective-permute-start | bytes 835592 | tf_op jit(solution)/shard_map/ppermute | solution.py:248
  56.9 0.1 reshape_squeeze.3
  57.0 0.6 gather_fusion
  57.6 0.1 broadcast_in_dim.8
  57.7 0.1 broadcast_in_dim_reshape.7.qrow_ref
  57.8 0.1 broadcast_in_dim.7
  57.9 0.2 broadcast_in_dim_reshape.8.kcol_ref
  58.1 14.9 %collective-permute-done.1.rest_0_ = bf16[2,272,256]{2,1,0:T(8,128)(2,1)S(1)} collective-permute-done((bf16[2,272,256]{2,1,0:T(8,128)(2,1)}, bf16[2,272,256]{2,1,0:T(8,128)(2,1)S(1)}, u32[]{:S(2)}, u32[]{:S(2)}) %collective-permute-start.1) | collective-permute-done | bytes 278560 | tf_op jit(solution)/shard_map/ppermute | solution.py:248
  73.0 43.7 %collective-permute-done.2.rest_1_ = bf16[2,272,256]{2,1,0:T(8,128)(2,1)S(1)} collective-permute-done((bf16[2,272,256]{2,1,0:T(8,128)(2,1)}, bf16[2,272,256]{2,1,0:T(8,128)(2,1)S(1)}, u32[]{:S(2)}, u32[]{:S(2)}) %collective-permute-start.2) | collective-permute-done | bytes 278560 | tf_op jit(solution)/shard_map/ppermute | solution.py:248
  116.7 0.0 collective-permute-done.3.rest_2_
  116.7 1.1 collective-permute-done.4.rest_3_
  117.7 0.0 all-to-all-done.kv_ref
  117.7 5.1 %attend.1 = (bf16[4,128,256]{2,1,0:T(8,128)(2,1)S(1)}, bf16[4,128,256]{2,1,0:T(8,128)(2,1)S(1)}, bf16[8,256,256]{2,1,0:T(8,128)(2,1)}) custom-call(bf16[8,256,256]{2,1,0:T(8,128)(2,1)S(1)} %all-to-all-done.kv_ref, s32[512,1]{1,0:T(8,128)S(1)} %broadcast_in_dim_reshape.8.kcol_ref, s32[1,512]{1,0:T(1,128)S(1)} %broadcast_in_dim_reshape.7.qrow_ref, ...), custom_call_target="tpu_custom_call" | custom-call | tf_op jit(solution)/shard_map/attend/pallas_call | solution.py:181
  122.8 0.7 copy-done
  123.5 16.6 %all-to-all-start.1 = ((bf16[8,256,256]{2,1,0:T(8,128)(2,1)}), bf16[8,256,256]{2,1,0:T(8,128)(2,1)S(1)}, u32[]{:S(2)}, u32[]{:S(2)}) async-start(bf16[8,256,256]{2,1,0:T(8,128)(2,1)} %get-tuple-element.26), calls=%async_computation.1 | async-start | bytes 2097152 | tf_op jit(solution)/shard_map/all_to_all | solution.py:257
  140.2 1.9 collective-permute-start.5
  142.1 1.5 collective-permute-done.5.x_ref
  143.6 0.7 copy-done.3
  144.3 1.8 pack_dq.1
  146.1 1.9 collective-permute-start.6
  148.0 1.9 collective-permute-start.7
  150.0 4.7 %collective-permute-start.8 = (bf16[2,128,256]{2,1,0:T(8,128)(2,1)}, bf16[2,128,256]{2,1,0:T(8,128)(2,1)S(1)}, u32[]{:S(2)}, u32[]{:S(2)}) collective-permute-start(bf16[2,128,256]{2,1,0:T(8,128)(2,1)} %get-tuple-element.24), channel_id=1, source_target_pairs={{508,0},{509,1},{510,2},{511,3},{504,4},{505,5},{506,6},{507,7},{4... | collective-permute-start | bytes 393224 | tf_op jit(solution)/shard_map/ppermute | solution.py:259
  154.7 7.9 %collective-permute-start.9 = (bf16[2,128,256]{2,1,0:T(8,128)(2,1)}, bf16[2,128,256]{2,1,0:T(8,128)(2,1)S(1)}, u32[]{:S(2)}, u32[]{:S(2)}) collective-permute-start(bf16[2,128,256]{2,1,0:T(8,128)(2,1)} %get-tuple-element.25), channel_id=1, source_target_pairs={{510,0},{511,1},{504,2},{505,3},{506,4},{507,5},{508,6},{509,7},{6... | collective-permute-start | bytes 393224 | tf_op jit(solution)/shard_map/ppermute | solution.py:259
  162.6 30.6 %collective-permute-done.6.rest_0_ = bf16[2,128,256]{2,1,0:T(8,128)(2,1)S(1)} collective-permute-done((bf16[2,128,256]{2,1,0:T(8,128)(2,1)}, bf16[2,128,256]{2,1,0:T(8,128)(2,1)S(1)}, u32[]{:S(2)}, u32[]{:S(2)}) %collective-permute-start.6) | collective-permute-done | bytes 131104 | tf_op jit(solution)/shard_map/ppermute | solution.py:259
  193.2 15.5 %collective-permute-done.7.rest_1_ = bf16[2,128,256]{2,1,0:T(8,128)(2,1)S(1)} collective-permute-done((bf16[2,128,256]{2,1,0:T(8,128)(2,1)}, bf16[2,128,256]{2,1,0:T(8,128)(2,1)S(1)}, u32[]{:S(2)}, u32[]{:S(2)}) %collective-permute-start.7) | collective-permute-done | bytes 131104 | tf_op jit(solution)/shard_map/ppermute | solution.py:259
  208.8 20.0 %collective-permute-done.8.rest_2_ = bf16[2,128,256]{2,1,0:T(8,128)(2,1)S(1)} collective-permute-done((bf16[2,128,256]{2,1,0:T(8,128)(2,1)}, bf16[2,128,256]{2,1,0:T(8,128)(2,1)S(1)}, u32[]{:S(2)}, u32[]{:S(2)}) %collective-permute-start.8) | collective-permute-done | bytes 131104 | tf_op jit(solution)/shard_map/ppermute | solution.py:259
  228.7 0.0 collective-permute-done.9.rest_3_
  228.7 0.6 copy-done.6
  229.4 0.6 copy-done.7
  230.0 2.1 unpack_q.1
  232.2 0.0 all-to-all-done.1.in_ref
  232.2 1.0 copy-done.1
  233.2 2.7 %unpack_kv.1 = (f32[128,2048]{1,0:T(8,128)}, f32[128,2048]{1,0:T(8,128)}) custom-call(bf16[8,256,256]{2,1,0:T(8,128)(2,1)} %copy-done.1), custom_call_target="tpu_custom_call" | custom-call | tf_op jit(solution)/shard_map/unpack_kv/pallas_call | solution.py:222
  (20 shorter events, 0.1 us)
Async XLA Ops:
  2.9 114.9 %all-to-all-start = ((bf16[8,256,256]{2,1,0:T(8,128)(2,1)}), bf16[8,256,256]{2,1,0:T(8,128)(2,1)S(1)}, u32[]{:S(2)}, u32[]{:S(2)}) async-start(bf16[8,256,256]{2,1,0:T(8,128)(2,1)} %pack_kv.1), calls=%async_computation | async-start | bytes 2097152 | tf_op jit(solution)/shard_map/all_to_all | solution.py:241
  15.9 0.7 copy-start.8
  16.6 0.7 copy-start.9
  20.7 4.0 %collective-permute-start = (bf16[4,272,256]{2,1,0:T(8,128)(2,1)}, bf16[4,272,256]{2,1,0:T(8,128)(2,1)S(1)}, u32[]{:S(2)}, u32[]{:S(2)}) collective-permute-start(bf16[4,272,256]{2,1,0:T(8,128)(2,1)} %pack_for_sibling.1), channel_id=1, source_target_pairs={{0,1},{1,0},{2,3},{3,2},{4,5},{5,4},{6,7},{7,6},{8,9},{9,8},{10,11... | collective-permute-start | bytes 1671176 | tf_op jit(solution)/shard_map/ppermute | solution.py:31
  24.7 0.8 copy-start.2
  28.0 28.8 %copy-start.10 = (s32[512,2]{0,1:T(2,128)S(1)}, s32[512,2]{0,1:T(2,128)}, u32[]{:S(2)}) copy-start(s32[512,2]{0,1:T(2,128)} %param.13) | copy-start | bytes 12292
  28.0 45.0 %collective-permute-start.1 = (bf16[2,272,256]{2,1,0:T(8,128)(2,1)}, bf16[2,272,256]{2,1,0:T(8,128)(2,1)S(1)}, u32[]{:S(2)}, u32[]{:S(2)}) collective-permute-start(bf16[2,272,256]{2,1,0:T(8,128)(2,1)} %get-tuple-element.16), channel_id=1, source_target_pairs={{0,504},{1,505},{2,506},{3,507},{4,508},{5,509},{6,510},{7,511},{8... | collective-permute-start | bytes 835592 | tf_op jit(solution)/shard_map/ppermute | solution.py:248
  35.4 81.3 %collective-permute-start.2 = (bf16[2,272,256]{2,1,0:T(8,128)(2,1)}, bf16[2,272,256]{2,1,0:T(8,128)(2,1)S(1)}, u32[]{:S(2)}, u32[]{:S(2)}) collective-permute-start(bf16[2,272,256]{2,1,0:T(8,128)(2,1)} %get-tuple-element.17), channel_id=1, source_target_pairs={{0,506},{1,507},{2,508},{3,509},{4,510},{5,511},{6,504},{7,505},{8... | collective-permute-start | bytes 835592 | tf_op jit(solution)/shard_map/ppermute | solution.py:248
  42.0 74.7 %collective-permute-start.3 = (bf16[2,272,256]{2,1,0:T(8,128)(2,1)}, bf16[2,272,256]{2,1,0:T(8,128)(2,1)S(1)}, u32[]{:S(2)}, u32[]{:S(2)}) collective-permute-start(bf16[2,272,256]{2,1,0:T(8,128)(2,1)} %get-tuple-element.18), channel_id=1, source_target_pairs={{0,508},{1,509},{2,510},{3,511},{4,504},{5,505},{6,506},{7,507},{8... | collective-permute-start | bytes 835592 | tf_op jit(solution)/shard_map/ppermute | solution.py:248
  48.9 68.8 %collective-permute-start.4 = (bf16[2,272,256]{2,1,0:T(8,128)(2,1)}, bf16[2,272,256]{2,1,0:T(8,128)(2,1)S(1)}, u32[]{:S(2)}, u32[]{:S(2)}) collective-permute-start(bf16[2,272,256]{2,1,0:T(8,128)(2,1)} %get-tuple-element.19), channel_id=1, source_target_pairs={{0,510},{1,511},{2,504},{3,505},{4,506},{5,507},{6,508},{7,509},{8... | collective-permute-start | bytes 835592 | tf_op jit(solution)/shard_map/ppermute | solution.py:248
  122.8 0.7 copy-start
  123.5 108.6 %all-to-all-start.1 = ((bf16[8,256,256]{2,1,0:T(8,128)(2,1)}), bf16[8,256,256]{2,1,0:T(8,128)(2,1)S(1)}, u32[]{:S(2)}, u32[]{:S(2)}) async-start(bf16[8,256,256]{2,1,0:T(8,128)(2,1)} %get-tuple-element.26), calls=%async_computation.1 | async-start | bytes 2097152 | tf_op jit(solution)/shard_map/all_to_all | solution.py:257
  140.2 3.4 %collective-permute-start.5 = (bf16[4,128,256]{2,1,0:T(8,128)(2,1)S(1)}, bf16[4,128,256]{2,1,0:T(8,128)(2,1)S(1)}, u32[]{:S(2)}, u32[]{:S(2)}) collective-permute-start(bf16[4,128,256]{2,1,0:T(8,128)(2,1)S(1)} %get-tuple-element.21), channel_id=1, source_target_pairs={{0,1},{1,0},{2,3},{3,2},{4,5},{5,4},{6,7},{7,6},{8,9},{9,8},{10,11... | collective-permute-start | bytes 786440 | tf_op jit(solution)/shard_map/ppermute | solution.py:31
  143.6 0.7 copy-start.3
  146.1 47.1 %collective-permute-start.6 = (bf16[2,128,256]{2,1,0:T(8,128)(2,1)}, bf16[2,128,256]{2,1,0:T(8,128)(2,1)S(1)}, u32[]{:S(2)}, u32[]{:S(2)}) collective-permute-start(bf16[2,128,256]{2,1,0:T(8,128)(2,1)} %get-tuple-element.22), channel_id=1, source_target_pairs={{504,0},{505,1},{506,2},{507,3},{508,4},{509,5},{510,6},{511,7},{0... | collective-permute-start | bytes 393224 | tf_op jit(solution)/shard_map/ppermute | solution.py:259
  148.0 60.7 %collective-permute-start.7 = (bf16[2,128,256]{2,1,0:T(8,128)(2,1)}, bf16[2,128,256]{2,1,0:T(8,128)(2,1)S(1)}, u32[]{:S(2)}, u32[]{:S(2)}) collective-permute-start(bf16[2,128,256]{2,1,0:T(8,128)(2,1)} %get-tuple-element.23), channel_id=1, source_target_pairs={{506,0},{507,1},{508,2},{509,3},{510,4},{511,5},{504,6},{505,7},{2... | collective-permute-start | bytes 393224 | tf_op jit(solution)/shard_map/ppermute | solution.py:259
  150.0 78.7 %collective-permute-start.8 = (bf16[2,128,256]{2,1,0:T(8,128)(2,1)}, bf16[2,128,256]{2,1,0:T(8,128)(2,1)S(1)}, u32[]{:S(2)}, u32[]{:S(2)}) collective-permute-start(bf16[2,128,256]{2,1,0:T(8,128)(2,1)} %get-tuple-element.24), channel_id=1, source_target_pairs={{508,0},{509,1},{510,2},{511,3},{504,4},{505,5},{506,6},{507,7},{4... | collective-permute-start | bytes 393224 | tf_op jit(solution)/shard_map/ppermute | solution.py:259
  154.7 74.0 %collective-permute-start.9 = (bf16[2,128,256]{2,1,0:T(8,128)(2,1)}, bf16[2,128,256]{2,1,0:T(8,128)(2,1)S(1)}, u32[]{:S(2)}, u32[]{:S(2)}) collective-permute-start(bf16[2,128,256]{2,1,0:T(8,128)(2,1)} %get-tuple-element.25), channel_id=1, source_target_pairs={{510,0},{511,1},{504,2},{505,3},{506,4},{507,5},{508,6},{509,7},{6... | collective-permute-start | bytes 393224 | tf_op jit(solution)/shard_map/ppermute | solution.py:259
  193.2 35.5 %copy-start.4 = (bf16[2,128,256]{2,1,0:T(8,128)(2,1)}, bf16[2,128,256]{2,1,0:T(8,128)(2,1)S(1)}, u32[]{:S(2)}) copy-start(bf16[2,128,256]{2,1,0:T(8,128)(2,1)S(1)} %collective-permute-done.6.rest_0_) | copy-start | bytes 393220
  208.8 20.0 %copy-start.5 = (bf16[2,128,256]{2,1,0:T(8,128)(2,1)}, bf16[2,128,256]{2,1,0:T(8,128)(2,1)S(1)}, u32[]{:S(2)}) copy-start(bf16[2,128,256]{2,1,0:T(8,128)(2,1)S(1)} %collective-permute-done.7.rest_1_) | copy-start | bytes 393220
  228.7 0.6 copy-start.6
  229.4 0.6 copy-start.7
  232.2 1.0 copy-start.1

commit v3 on v2

--- a/solution.py
+++ b/solution.py
@@ -11,20 +11,39 @@
 STAT_ROWS = 16
 LOG2E = 1.4426950408889634
 CHIPS = 4
-
-
-def moved_inner(i, dz, dc, sign=1):
-    return ((i // 2 + sign * dz) % 4) * 2 + (i + dc) % 2
-
-
-def send_pairs(outer_count, dz, back):
+TURNS = (2, 1, 3, 0)
+PLANE = 16
+
+
+def moved_inner(i, dz, dc):
+    return ((i // 2 + dz) % CHIPS) * 2 + (i + dc) % 2
+
+
+def source_turn(o, dz):
+    return dz - 1 if o == 0 else dz
+
+
+def send_pairs(outer_count, dz, back, crossing=True):
     pairs = []
     for o in range(outer_count):
+        if o % PLANE == 0 and not crossing:
+            continue
         for i in range(N_INNER):
             here = o * N_INNER + i
-            there = ((o - 1) % outer_count) * N_INNER + moved_inner(i, dz, 0)
+            there = ((o - 1) % outer_count) * N_INNER + moved_inner(i, source_turn(o, dz), 0)
             pairs.append((there, here) if back else (here, there))
     return pairs
+
+
+def long_way(outer_count):
+    first, second = [], []
+    for o in range(0, outer_count, PLANE):
+        for i in range(N_INNER):
+            far = moved_inner(i, source_turn(o, TURNS[0]), 0)
+            middle = o * N_INNER + moved_inner(i, -1, 0)
+            first.append((o * N_INNER + i, middle))
+            second.append((middle, ((o - 1) % outer_count) * N_INNER + far))
+    return first, second
 
 
 def to_sibling(x):
@@ -79,15 +98,23 @@
 
 def pack_q(chunk, queries, grad_out, stats, from_sibling):
     rows = queries.shape[0]
+    whole = 2 * rows + STAT_ROWS
 
     def kernel(chunk_ref, q_ref, o_ref, s_ref, x_ref, *outs):
-        for dz, out in enumerate(outs):
-            chunk_of(q_ref, o_ref, s_ref, chunk_ref[2 * dz], out, (0,))
-            out[1] = x_ref[dz]
-
-    return pl.pallas_call(
-        kernel,
-        out_shape=[jax.ShapeDtypeStruct((2, 2 * rows + STAT_ROWS, PAIR), queries.dtype)] * CHIPS,
+        short = outs[0]
+        j = chunk_ref[0]
+        cols = pl.ds(pl.multiple_of(j * PAIR, PAIR), PAIR)
+        short[pl.ds(0, rows), :] = q_ref[:, cols]
+        short[pl.ds(rows, STAT_ROWS), :] = s_ref[j]
+        short[pl.ds(rows + STAT_ROWS, whole), :] = x_ref[0]
+        for t in range(1, CHIPS):
+            chunk_of(q_ref, o_ref, s_ref, chunk_ref[2 * t], outs[t], (0,))
+            outs[t][1] = x_ref[t]
+
+    return pl.pallas_call(
+        kernel,
+        out_shape=[jax.ShapeDtypeStruct((rows + STAT_ROWS + whole, PAIR), queries.dtype)]
+        + [jax.ShapeDtypeStruct((2, whole, PAIR), queries.dtype)] * (CHIPS - 1),
         in_specs=[SMEM] + [VMEM] * 4,
         out_specs=[VMEM] * CHIPS,
         name="pack_q",
@@ -96,9 +123,9 @@
 
 def pack_dq(own, from_sibling):
     def kernel(own_ref, x_ref, *outs):
-        for dz, out in enumerate(outs):
-            out[0] = own_ref[dz]
-            out[1] = x_ref[dz]
+        for t, out in enumerate(outs):
+            out[0] = own_ref[t]
+            out[1] = x_ref[t]
 
     return pl.pallas_call(
         kernel,
@@ -109,27 +136,34 @@
     )(own, from_sibling)
 
 
-def attend(kv, parts, kcol, qrow):
+def attend(kv, parts, slice_o, kcol, qrow):
     rows = kv.shape[1] // 2
     half = rows // 2
     side = N_INNER * half
     scale = WIDTH ** -0.5
     tile = 256
 
-    def kernel(kv_ref, kcol_ref, qrow_ref, *rest):
+    def kernel(kv_ref, kcol_ref, qrow_ref, slice_ref, *rest):
         ins, rest = rest[:CHIPS], rest[CHIPS:]
-        ins = [ins[a // 2].at[a % 2] for a in range(N_INNER)]
+        from_start = (0, rows, 2 * rows)
+        blocks = [(ins[a // 2].at[a % 2], from_start) for a in range(2, N_INNER)]
+        after = rows + STAT_ROWS
+        blocks = [(ins[0], (0, None, rows)), (ins[0], tuple(after + r for r in from_start))] + blocks
         dqs = [rest[a % 2].at[a // 2] for a in range(N_INNER)]
         dkv_ref, q_s, o_s, k_s, v_s, l_s, d_s, dk_s, dv_s = rest[2:]
         for a in range(N_INNER):
+            ref, (q_at, o_at, s_at) = blocks[a]
             for part in range(2):
                 to = pl.ds(part * side + a * half, half)
                 at = part * half
-                q_s[to, :] = ins[a][pl.ds(at, half), :]
-                o_s[to, :] = ins[a][pl.ds(rows + at, half), :]
+                q_s[to, :] = ref[pl.ds(q_at + at, half), :]
+                if o_at is None:
+                    o_s[to, :] = slice_ref[pl.ds(at, half), :]
+                else:
+                    o_s[to, :] = ref[pl.ds(o_at + at, half), :]
                 k_s[to, :] = kv_ref[a, pl.ds(at, half), :]
                 v_s[to, :] = kv_ref[a, pl.ds(rows + at, half), :]
-            st = ins[a][pl.ds(2 * rows, STAT_ROWS), :].astype(jnp.float32)
+            st = ref[pl.ds(s_at, STAT_ROWS), :].astype(jnp.float32)
             for h in range(2):
                 for part in range(2):
                     lanes = slice(h * WIDTH + part * half, h * WIDTH + (part + 1) * half)
@@ -182,14 +216,14 @@
         kernel,
         out_shape=[jax.ShapeDtypeStruct((CHIPS, rows, PAIR), jnp.bfloat16)] * 2
         + [jax.ShapeDtypeStruct(kv.shape, jnp.bfloat16)],
-        in_specs=[VMEM] * (3 + CHIPS),
+        in_specs=[VMEM] * (4 + CHIPS),
         out_specs=[VMEM] * 3,
         scratch_shapes=[pltpu.VMEM((2 * side, PAIR), jnp.bfloat16)] * 4
         + [pltpu.VMEM((2, 2 * side), jnp.float32)] * 2
         + [pltpu.VMEM((2 * side, WIDTH), jnp.float32)] * 2,
         compiler_params=pltpu.CompilerParams(vmem_limit_bytes=40 * 1024 * 1024),
         name="attend",
-    )(kv, kcol, qrow, *parts)
+    )(kv, kcol, qrow, slice_o, *parts)
 
 
 def unpack_q(chunk, parts):
@@ -234,18 +268,26 @@
     inner_idx = lax.axis_index("inner")
     rows = queries.shape[0]
     half = rows // 2
-    turns = [(dz, dc) for dz in range(CHIPS) for dc in range(2)]
-    chunk = jnp.stack([moved_inner(inner_idx, *t) for t in turns]).astype(jnp.int32)
-    senders = jnp.stack([moved_inner(inner_idx, *t, -1) for t in turns]).astype(jnp.int32)
+    to_wrap = (outer_idx == 0).astype(jnp.int32)
+    from_wrap = (outer_idx == outer_count - 1).astype(jnp.int32)
+    chunk = jnp.stack([moved_inner(inner_idx, dz - to_wrap, dc) for dz in TURNS for dc in range(2)])
+    senders = jnp.stack([moved_inner(inner_idx, from_wrap - dz, dc) for dz in TURNS for dc in range(2)])
+
+    axes = ("outer", "inner")
+    first_leg, second_leg = long_way(outer_count)
 
     kv = lax.all_to_all(pack_kv(keys, values), "inner", 0, 0, tiled=True)
+
+    slice_o = lax.dynamic_slice_in_dim(grad_out, chunk[0] * PAIR, PAIR, 1)
+    middle = lax.ppermute(slice_o, axes, first_leg)
+    slice_o = jnp.where(outer_idx % PLANE == 0, middle, slice_o)
 
     stats = jnp.stack([lse.T.reshape(N_INNER, PAIR), delta.T.reshape(N_INNER, PAIR)], axis=1)
     stats = jnp.pad(stats, ((0, 0), (0, STAT_ROWS - 2), (0, 0)))
     crossed = to_sibling(pack_for_sibling(chunk, queries, grad_out, stats))
     sent = pack_q(chunk, queries, grad_out, stats, crossed)
-    axes = ("outer", "inner")
-    parts = [lax.ppermute(x, axes, send_pairs(outer_count, dz, False)) for dz, x in enumerate(sent)]
+    slice_o = lax.ppermute(slice_o, axes, send_pairs(outer_count, TURNS[0], False, crossing=False) + second_leg)
+    parts = [lax.ppermute(x, axes, send_pairs(outer_count, dz, False)) for dz, x in zip(TURNS, sent)]
 
     first = span_table[:, 0].reshape(outer_count, N_INNER)
     key_c = lax.dynamic_index_in_dim(first, outer_idx, 0, keepdims=False)
@@ -253,11 +295,12 @@
     kcol = jnp.repeat(key_c, half)[:, None]
     qrow = jnp.repeat(query_c, half)[None, :]
 
-    own_dq, sibling_dq, dkv = attend(kv, parts, kcol, qrow)
+    own_dq, sibling_dq, dkv = attend(kv, parts, slice_o, kcol, qrow)
     dkv = lax.all_to_all(dkv, "inner", 0, 0, tiled=True)
     sent = pack_dq(own_dq, to_sibling(sibling_dq))
-    back = [lax.ppermute(x, axes, send_pairs(outer_count, dz, True)) for dz, x in enumerate(sent)]
+    back = [lax.ppermute(x, axes, send_pairs(outer_count, dz, True)) for dz, x in zip(TURNS, sent)]
     grad_k, grad_v = unpack_kv(dkv)
+    back, grad_k, grad_v = lax.optimization_barrier((back, grad_k, grad_v))
     grad_q = unpack_q(chunk, back)
     return grad_q, grad_k, grad_v
 

time: 237 us -> 220 us (0.928)
  the two profiles are of different devices: /device:TPU:97 before, /device:TPU:33 now
where the time goes in v3:
time: 220 us; the launch traced here: 219 us
  waiting for transfers between devices  103 us (47%)
  starting transfers between devices  87.2 us (40%)
  Pallas kernels  18.5 us (8%)
  local copies, waits for them, and re-layouts  8.7 us (4%)
    ppermute x4, waiting for transfers between devices, shards(): lax.ppermute(x, axes, send_pairs(outer_count, dz, True))  49.8 us
    ppermute x1, waiting for transfers between devices, shards(): lax.ppermute(slice_o, axes, send_pairs(outer_count, TURNS[0], False, cros...  37.1 us
    ppermute x4, starting transfers between devices, shards(): lax.ppermute(x, axes, send_pairs(outer_count, dz, True))  27.4 us
    ppermute x4, starting transfers between devices, shards(): lax.ppermute(x, axes, send_pairs(outer_count, dz, False))  22.1 us
    all_to_all x1, starting transfers between devices, shards(): kv = lax.all_to_all(pack_kv(keys, values), 'inner', 0, 0, tiled=True)  14.9 us
    ppermute x1, waiting for transfers between devices, shards(): middle = lax.ppermute(slice_o, axes, first_leg)  14.2 us
    all_to_all x1, starting transfers between devices, shards(): dkv = lax.all_to_all(dkv, 'inner', 0, 0, tiled=True)  9.52 us
    ppermute x1, starting transfers between devices, shards(): middle = lax.ppermute(slice_o, axes, first_leg)  7.54 us
  transfers between devices with their start and end apart: 14, of which 5 were waited for; matrix products, arithmetic and copies ran while one was open for 2% of the time, Pallas kernels for 4%

profile of v3, /device:TPU:33, one launch (start us, length us, event | category | flops | bytes accessed | tf_op | source)
XLA Modules:
  0.0 219.4 jit_solution(8728933002777375633)
XLA Ops:
  0.6 2.2 %pack_kv.1 = bf16[8,256,256]{2,1,0:T(8,128)(2,1)} custom-call(bf16[128,2048]{1,0:T(8,128)(2,1)} %k_ref.1, bf16[128,2048]{1,0:T(8,128)(2,1)} %v_ref.1), custom_call_target="tpu_custom_call" | custom-call | tf_op jit(solution)/shard_map/pack_kv/pallas_call | solution.py:66
  2.9 14.9 %all-to-all-start = ((bf16[8,256,256]{2,1,0:T(8,128)(2,1)}), bf16[8,256,256]{2,1,0:T(8,128)(2,1)S(1)}, u32[]{:S(2)}, u32[]{:S(2)}) async-start(bf16[8,256,256]{2,1,0:T(8,128)(2,1)} %pack_kv.1), calls=%async_computation | async-start | bytes 2097152 | tf_op jit(solution)/shard_map/all_to_all | solution.py:279
  17.7 0.7 copy-done.8
  18.4 0.7 copy-done.9
  19.1 0.6 stack.65.chunk_ref
  19.7 0.7 fusion.2.s_ref
  20.4 2.1 pack_for_sibling.1
  22.5 1.9 collective-permute-start.2
  24.4 0.8 constant_dynamic-slice_fusion
  25.3 7.5 %collective-permute-start = (bf16[128,256]{1,0:T(8,128)(2,1)S(1)}, bf16[128,256]{1,0:T(8,128)(2,1)S(1)}, u32[]{:S(2)}, u32[]{:S(2)}) collective-permute-start(bf16[128,256]{1,0:T(8,128)(2,1)S(1)} %constant_dynamic-slice_fusion), channel_id=1, source_target_pairs={{0,6},{1,7},{2,0},{3,1},{4,2},{5,3},{6,4},{7,5},{128,134},{129,135... | collective-permute-start | bytes 196616 | tf_op jit(solution)/shard_map/ppermute | solution.py:282
  32.9 0.0 copy-start.10
  32.9 0.7 copy-done.10
  33.6 0.1 reshape_squeeze.3
  33.7 0.1 stack.74
  33.9 0.8 copy-done.2
  34.7 2.4 %pack_q.1 = (bf16[416,256]{1,0:T(8,128)(2,1)}, bf16[2,272,256]{2,1,0:T(8,128)(2,1)}, bf16[2,272,256]{2,1,0:T(8,128)(2,1)}, bf16[2,272,256]{2,1,0:T(8,128)(2,1)}) custom-call(s32[8]{0:T(128)} %stack.65.chunk_ref, bf16[128,2048]{1,0:T(8,128)(2,1)} %q_ref.3, bf16[128,2048]{1,0:T(8,128)(2,1)} %o_ref.3, bf16[8,16,256]{2,1,0:T(8,128)(2,1)} %fusion.2.s_ref, ...), custom_call_target="tpu_custom_call" | custom-call | tf_op jit(solution)/shard_map/pack_q/pallas_call | solution.py:114
  37.1 9.6 %collective-permute-start.3 = (bf16[416,256]{1,0:T(8,128)(2,1)}, bf16[416,256]{1,0:T(8,128)(2,1)S(1)}, u32[]{:S(2)}, u32[]{:S(2)}) collective-permute-start(bf16[416,256]{1,0:T(8,128)(2,1)} %get-tuple-element.22), channel_id=1, source_target_pairs={{0,506},{1,507},{2,508},{3,509},{4,510},{5,511},{6,504},{7,505},{8... | collective-permute-start | bytes 638984 | tf_op jit(solution)/shard_map/ppermute | solution.py:290
  46.7 2.5 %collective-permute-start.4 = (bf16[2,272,256]{2,1,0:T(8,128)(2,1)}, bf16[2,272,256]{2,1,0:T(8,128)(2,1)S(1)}, u32[]{:S(2)}, u32[]{:S(2)}) collective-permute-start(bf16[2,272,256]{2,1,0:T(8,128)(2,1)} %get-tuple-element.23), channel_id=1, source_target_pairs={{0,504},{1,505},{2,506},{3,507},{4,508},{5,509},{6,510},{7,511},{8... | collective-permute-start | bytes 835592 | tf_op jit(solution)/shard_map/ppermute | solution.py:290
  49.2 7.9 %collective-permute-start.5 = (bf16[2,272,256]{2,1,0:T(8,128)(2,1)}, bf16[2,272,256]{2,1,0:T(8,128)(2,1)S(1)}, u32[]{:S(2)}, u32[]{:S(2)}) collective-permute-start(bf16[2,272,256]{2,1,0:T(8,128)(2,1)} %get-tuple-element.24), channel_id=1, source_target_pairs={{0,508},{1,509},{2,510},{3,511},{4,504},{5,505},{6,506},{7,507},{8... | collective-permute-start | bytes 835592 | tf_op jit(solution)/shard_map/ppermute | solution.py:290
  57.1 2.2 collective-permute-start.6
  59.2 14.2 %collective-permute-done = bf16[128,256]{1,0:T(8,128)(2,1)S(1)} collective-permute-done((bf16[128,256]{1,0:T(8,128)(2,1)S(1)}, bf16[128,256]{1,0:T(8,128)(2,1)S(1)}, u32[]{:S(2)}, u32[]{:S(2)}) %collective-permute-start) | collective-permute-done | bytes 65568 | tf_op jit(solution)/shard_map/ppermute | solution.py:282
  73.4 0.9 broadcast_select_fusion
  74.3 1.9 collective-permute-start.1
  76.2 0.6 gather_fusion
  76.8 0.1 broadcast_in_dim.8
  76.9 0.1 broadcast_in_dim_reshape.7.qrow_ref
  77.0 0.1 broadcast_in_dim.7
  77.1 0.2 broadcast_in_dim_reshape.8.kcol_ref
  77.3 37.1 %collective-permute-done.1.slice_ref = bf16[128,256]{1,0:T(8,128)(2,1)S(1)} collective-permute-done((bf16[128,256]{1,0:T(8,128)(2,1)S(1)}, bf16[128,256]{1,0:T(8,128)(2,1)S(1)}, u32[]{:S(2)}, u32[]{:S(2)}) %collective-permute-start.1) | collective-permute-done | bytes 65568 | tf_op jit(solution)/shard_map/ppermute | solution.py:289
  114.4 5.1 %attend.1 = (bf16[4,128,256]{2,1,0:T(8,128)(2,1)S(1)}, bf16[4,128,256]{2,1,0:T(8,128)(2,1)S(1)}, bf16[8,256,256]{2,1,0:T(8,128)(2,1)}) custom-call(bf16[8,256,256]{2,1,0:T(8,128)(2,1)S(1)} %all-to-all-done.kv_ref, s32[512,1]{1,0:T(8,128)S(1)} %broadcast_in_dim_reshape.8.kcol_ref, s32[1,512]{1,0:T(1,128)S(1)} %broadcast_in_dim_reshape.7.qrow_ref, ...), custom_call_target="tpu_custom_call" | custom-call | tf_op jit(solution)/shard_map/attend/pallas_call | solution.py:215
  119.5 0.7 copy-done
  120.2 9.5 %all-to-all-start.1 = ((bf16[8,256,256]{2,1,0:T(8,128)(2,1)}), bf16[8,256,256]{2,1,0:T(8,128)(2,1)S(1)}, u32[]{:S(2)}, u32[]{:S(2)}) async-start(bf16[8,256,256]{2,1,0:T(8,128)(2,1)} %get-tuple-element.32), calls=%async_computation.1 | async-start | bytes 2097152 | tf_op jit(solution)/shard_map/all_to_all | solution.py:299
  129.7 1.9 collective-permute-start.7
  131.6 1.5 collective-permute-done.7.x_ref
  133.1 0.7 copy-done.3
  133.8 1.9 pack_dq.1
  135.7 13.4 %collective-permute-start.8 = (bf16[2,128,256]{2,1,0:T(8,128)(2,1)}, bf16[2,128,256]{2,1,0:T(8,128)(2,1)S(1)}, u32[]{:S(2)}, u32[]{:S(2)}) collective-permute-start(bf16[2,128,256]{2,1,0:T(8,128)(2,1)} %get-tuple-element.28), channel_id=1, source_target_pairs={{506,0},{507,1},{508,2},{509,3},{510,4},{511,5},{504,6},{505,7},{4... | collective-permute-start | bytes 393224 | tf_op jit(solution)/shard_map/ppermute | solution.py:301
  149.1 3.0 %collective-permute-start.9 = (bf16[2,128,256]{2,1,0:T(8,128)(2,1)}, bf16[2,128,256]{2,1,0:T(8,128)(2,1)S(1)}, u32[]{:S(2)}, u32[]{:S(2)}) collective-permute-start(bf16[2,128,256]{2,1,0:T(8,128)(2,1)} %get-tuple-element.29), channel_id=1, source_target_pairs={{504,0},{505,1},{506,2},{507,3},{508,4},{509,5},{510,6},{511,7},{2... | collective-permute-start | bytes 393224 | tf_op jit(solution)/shard_map/ppermute | solution.py:301
  152.1 8.0 %collective-permute-start.10 = (bf16[2,128,256]{2,1,0:T(8,128)(2,1)}, bf16[2,128,256]{2,1,0:T(8,128)(2,1)S(1)}, u32[]{:S(2)}, u32[]{:S(2)}) collective-permute-start(bf16[2,128,256]{2,1,0:T(8,128)(2,1)} %get-tuple-element.30), channel_id=1, source_target_pairs={{508,0},{509,1},{510,2},{511,3},{504,4},{505,5},{506,6},{507,7},{6... | collective-permute-start | bytes 393224 | tf_op jit(solution)/shard_map/ppermute | solution.py:301
  160.2 2.9 %collective-permute-start.11 = (bf16[2,128,256]{2,1,0:T(8,128)(2,1)}, bf16[2,128,256]{2,1,0:T(8,128)(2,1)S(1)}, u32[]{:S(2)}, u32[]{:S(2)}) collective-permute-start(bf16[2,128,256]{2,1,0:T(8,128)(2,1)} %get-tuple-element.31), channel_id=1, source_target_pairs={{510,0},{511,1},{504,2},{505,3},{506,4},{507,5},{508,6},{509,7},{0... | collective-permute-start | bytes 393224 | tf_op jit(solution)/shard_map/ppermute | solution.py:301
  163.1 1.0 copy-done.1
  164.1 2.7 %unpack_kv.1 = (f32[128,2048]{1,0:T(8,128)}, f32[128,2048]{1,0:T(8,128)}) custom-call(bf16[8,256,256]{2,1,0:T(8,128)(2,1)} %copy-done.1), custom_call_target="tpu_custom_call" | custom-call | tf_op jit(solution)/shard_map/unpack_kv/pallas_call | solution.py:256
  166.8 44.1 %collective-permute-done.8.rest_0_ = bf16[2,128,256]{2,1,0:T(8,128)(2,1)S(1)} collective-permute-done((bf16[2,128,256]{2,1,0:T(8,128)(2,1)}, bf16[2,128,256]{2,1,0:T(8,128)(2,1)S(1)}, u32[]{:S(2)}, u32[]{:S(2)}) %collective-permute-start.8) | collective-permute-done | bytes 131104 | tf_op jit(solution)/shard_map/ppermute | solution.py:301
  210.8 5.7 %collective-permute-done.9.rest_1_ = bf16[2,128,256]{2,1,0:T(8,128)(2,1)S(1)} collective-permute-done((bf16[2,128,256]{2,1,0:T(8,128)(2,1)}, bf16[2,128,256]{2,1,0:T(8,128)(2,1)S(1)}, u32[]{:S(2)}, u32[]{:S(2)}) %collective-permute-start.9) | collective-permute-done | bytes 131104 | tf_op jit(solution)/shard_map/ppermute | solution.py:301
  216.6 0.6 copy-done.5
  217.2 0.1 copy-done.6
  217.2 0.0 copy-done.7
  217.3 2.1 unpack_q.1
  (26 shorter events, 0.1 us)
Async XLA Ops:
  2.9 111.5 %all-to-all-start = ((bf16[8,256,256]{2,1,0:T(8,128)(2,1)}), bf16[8,256,256]{2,1,0:T(8,128)(2,1)S(1)}, u32[]{:S(2)}, u32[]{:S(2)}) async-start(bf16[8,256,256]{2,1,0:T(8,128)(2,1)} %pack_kv.1), calls=%async_computation | async-start | bytes 2097152 | tf_op jit(solution)/shard_map/all_to_all | solution.py:279
  17.7 0.7 copy-start.8
  18.4 0.7 copy-start.9
  22.5 11.4 %collective-permute-start.2 = (bf16[4,272,256]{2,1,0:T(8,128)(2,1)}, bf16[4,272,256]{2,1,0:T(8,128)(2,1)S(1)}, u32[]{:S(2)}, u32[]{:S(2)}) collective-permute-start(bf16[4,272,256]{2,1,0:T(8,128)(2,1)} %pack_for_sibling.1), channel_id=1, source_target_pairs={{0,1},{1,0},{2,3},{3,2},{4,5},{5,4},{6,7},{7,6},{8,9},{9,8},{10,11... | collective-permute-start | bytes 1671176 | tf_op jit(solution)/shard_map/ppermute | solution.py:50
  25.3 48.1 %collective-permute-start = (bf16[128,256]{1,0:T(8,128)(2,1)S(1)}, bf16[128,256]{1,0:T(8,128)(2,1)S(1)}, u32[]{:S(2)}, u32[]{:S(2)}) collective-permute-start(bf16[128,256]{1,0:T(8,128)(2,1)S(1)} %constant_dynamic-slice_fusion), channel_id=1, source_target_pairs={{0,6},{1,7},{2,0},{3,1},{4,2},{5,3},{6,4},{7,5},{128,134},{129,135... | collective-permute-start | bytes 196616 | tf_op jit(solution)/shard_map/ppermute | solution.py:282
  32.9 0.7 copy-start.10
  33.9 0.8 copy-start.2
  37.1 77.3 %collective-permute-start.3 = (bf16[416,256]{1,0:T(8,128)(2,1)}, bf16[416,256]{1,0:T(8,128)(2,1)S(1)}, u32[]{:S(2)}, u32[]{:S(2)}) collective-permute-start(bf16[416,256]{1,0:T(8,128)(2,1)} %get-tuple-element.22), channel_id=1, source_target_pairs={{0,506},{1,507},{2,508},{3,509},{4,510},{5,511},{6,504},{7,505},{8... | collective-permute-start | bytes 638984 | tf_op jit(solution)/shard_map/ppermute | solution.py:290
  46.7 67.6 %collective-permute-start.4 = (bf16[2,272,256]{2,1,0:T(8,128)(2,1)}, bf16[2,272,256]{2,1,0:T(8,128)(2,1)S(1)}, u32[]{:S(2)}, u32[]{:S(2)}) collective-permute-start(bf16[2,272,256]{2,1,0:T(8,128)(2,1)} %get-tuple-element.23), channel_id=1, source_target_pairs={{0,504},{1,505},{2,506},{3,507},{4,508},{5,509},{6,510},{7,511},{8... | collective-permute-start | bytes 835592 | tf_op jit(solution)/shard_map/ppermute | solution.py:290
  49.2 65.2 %collective-permute-start.5 = (bf16[2,272,256]{2,1,0:T(8,128)(2,1)}, bf16[2,272,256]{2,1,0:T(8,128)(2,1)S(1)}, u32[]{:S(2)}, u32[]{:S(2)}) collective-permute-start(bf16[2,272,256]{2,1,0:T(8,128)(2,1)} %get-tuple-element.24), channel_id=1, source_target_pairs={{0,508},{1,509},{2,510},{3,511},{4,504},{5,505},{6,506},{7,507},{8... | collective-permute-start | bytes 835592 | tf_op jit(solution)/shard_map/ppermute | solution.py:290
  57.1 57.3 %collective-permute-start.6 = (bf16[2,272,256]{2,1,0:T(8,128)(2,1)}, bf16[2,272,256]{2,1,0:T(8,128)(2,1)S(1)}, u32[]{:S(2)}, u32[]{:S(2)}) collective-permute-start(bf16[2,272,256]{2,1,0:T(8,128)(2,1)} %get-tuple-element.25), channel_id=1, source_target_pairs={{0,510},{1,511},{2,504},{3,505},{4,506},{5,507},{6,508},{7,509},{8... | collective-permute-start | bytes 835592 | tf_op jit(solution)/shard_map/ppermute | solution.py:290
  74.3 40.1 %collective-permute-start.1 = (bf16[128,256]{1,0:T(8,128)(2,1)S(1)}, bf16[128,256]{1,0:T(8,128)(2,1)S(1)}, u32[]{:S(2)}, u32[]{:S(2)}) collective-permute-start(bf16[128,256]{1,0:T(8,128)(2,1)S(1)} %broadcast_select_fusion), channel_id=1, source_target_pairs={{8,4},{9,5},{10,6},{11,7},{12,0},{13,1},{14,2},{15,3},{16,12},{17,... | collective-permute-start | bytes 196616 | tf_op jit(solution)/shard_map/ppermute | solution.py:289
  119.5 0.7 copy-start
  120.2 42.9 %all-to-all-start.1 = ((bf16[8,256,256]{2,1,0:T(8,128)(2,1)}), bf16[8,256,256]{2,1,0:T(8,128)(2,1)S(1)}, u32[]{:S(2)}, u32[]{:S(2)}) async-start(bf16[8,256,256]{2,1,0:T(8,128)(2,1)} %get-tuple-element.32), calls=%async_computation.1 | async-start | bytes 2097152 | tf_op jit(solution)/shard_map/all_to_all | solution.py:299
  129.7 3.4 %collective-permute-start.7 = (bf16[4,128,256]{2,1,0:T(8,128)(2,1)S(1)}, bf16[4,128,256]{2,1,0:T(8,128)(2,1)S(1)}, u32[]{:S(2)}, u32[]{:S(2)}) collective-permute-start(bf16[4,128,256]{2,1,0:T(8,128)(2,1)S(1)} %get-tuple-element.27), channel_id=1, source_target_pairs={{0,1},{1,0},{2,3},{3,2},{4,5},{5,4},{6,7},{7,6},{8,9},{9,8},{10,11... | collective-permute-start | bytes 786440 | tf_op jit(solution)/shard_map/ppermute | solution.py:50
  133.1 0.7 copy-start.3
  135.7 75.2 %collective-permute-start.8 = (bf16[2,128,256]{2,1,0:T(8,128)(2,1)}, bf16[2,128,256]{2,1,0:T(8,128)(2,1)S(1)}, u32[]{:S(2)}, u32[]{:S(2)}) collective-permute-start(bf16[2,128,256]{2,1,0:T(8,128)(2,1)} %get-tuple-element.28), channel_id=1, source_target_pairs={{506,0},{507,1},{508,2},{509,3},{510,4},{511,5},{504,6},{505,7},{4... | collective-permute-start | bytes 393224 | tf_op jit(solution)/shard_map/ppermute | solution.py:301
  149.1 67.4 %collective-permute-start.9 = (bf16[2,128,256]{2,1,0:T(8,128)(2,1)}, bf16[2,128,256]{2,1,0:T(8,128)(2,1)S(1)}, u32[]{:S(2)}, u32[]{:S(2)}) collective-permute-start(bf16[2,128,256]{2,1,0:T(8,128)(2,1)} %get-tuple-element.29), channel_id=1, source_target_pairs={{504,0},{505,1},{506,2},{507,3},{508,4},{509,5},{510,6},{511,7},{2... | collective-permute-start | bytes 393224 | tf_op jit(solution)/shard_map/ppermute | solution.py:301
  152.1 64.4 %collective-permute-start.10 = (bf16[2,128,256]{2,1,0:T(8,128)(2,1)}, bf16[2,128,256]{2,1,0:T(8,128)(2,1)S(1)}, u32[]{:S(2)}, u32[]{:S(2)}) collective-permute-start(bf16[2,128,256]{2,1,0:T(8,128)(2,1)} %get-tuple-element.30), channel_id=1, source_target_pairs={{508,0},{509,1},{510,2},{511,3},{504,4},{505,5},{506,6},{507,7},{6... | collective-permute-start | bytes 393224 | tf_op jit(solution)/shard_map/ppermute | solution.py:301
  160.2 56.4 %collective-permute-start.11 = (bf16[2,128,256]{2,1,0:T(8,128)(2,1)}, bf16[2,128,256]{2,1,0:T(8,128)(2,1)S(1)}, u32[]{:S(2)}, u32[]{:S(2)}) collective-permute-start(bf16[2,128,256]{2,1,0:T(8,128)(2,1)} %get-tuple-element.31), channel_id=1, source_target_pairs={{510,0},{511,1},{504,2},{505,3},{506,4},{507,5},{508,6},{509,7},{0... | collective-permute-start | bytes 393224 | tf_op jit(solution)/shard_map/ppermute | solution.py:301
  163.1 1.0 copy-start.1
  210.8 5.7 %copy-start.4 = (bf16[2,128,256]{2,1,0:T(8,128)(2,1)}, bf16[2,128,256]{2,1,0:T(8,128)(2,1)S(1)}, u32[]{:S(2)}) copy-start(bf16[2,128,256]{2,1,0:T(8,128)(2,1)S(1)} %collective-permute-done.8.rest_0_) | copy-start | bytes 393220
  216.5 0.6 copy-start.5
  216.5 0.7 copy-start.6
  216.5 0.7 copy-start.7

commit v4 on v3

--- a/solution.py
+++ b/solution.py
@@ -35,14 +35,23 @@
     return pairs
 
 
-def long_way(outer_count):
+def long_way(outer_count, back):
     first, second = [], []
+    planes = outer_count // PLANE
     for o in range(0, outer_count, PLANE):
+        owner = (o - 1) % outer_count
         for i in range(N_INNER):
             far = moved_inner(i, source_turn(o, TURNS[0]), 0)
-            middle = o * N_INNER + moved_inner(i, -1, 0)
-            first.append((o * N_INNER + i, middle))
-            second.append((middle, ((o - 1) % outer_count) * N_INNER + far))
+            here, there = o * N_INNER + i, owner * N_INNER + far
+            if back:
+                z = (far // 2 * planes + owner // PLANE + 2) % (planes * CHIPS)
+                middle = (z % planes * PLANE + PLANE - 1) * N_INNER + z // planes * 2 + far % 2
+                here, there = there, here
+            else:
+                z = (i // 2 * planes + o // PLANE - 2) % (planes * CHIPS)
+                middle = z % planes * PLANE * N_INNER + z // planes * 2 + i % 2
+            first.append((here, middle))
+            second.append((middle, there))
     return first, second
 
 
@@ -98,23 +107,24 @@
 
 def pack_q(chunk, queries, grad_out, stats, from_sibling):
     rows = queries.shape[0]
-    whole = 2 * rows + STAT_ROWS
 
     def kernel(chunk_ref, q_ref, o_ref, s_ref, x_ref, *outs):
-        short = outs[0]
-        j = chunk_ref[0]
-        cols = pl.ds(pl.multiple_of(j * PAIR, PAIR), PAIR)
-        short[pl.ds(0, rows), :] = q_ref[:, cols]
-        short[pl.ds(rows, STAT_ROWS), :] = s_ref[j]
-        short[pl.ds(rows + STAT_ROWS, whole), :] = x_ref[0]
-        for t in range(1, CHIPS):
-            chunk_of(q_ref, o_ref, s_ref, chunk_ref[2 * t], outs[t], (0,))
-            outs[t][1] = x_ref[t]
-
-    return pl.pallas_call(
-        kernel,
-        out_shape=[jax.ShapeDtypeStruct((rows + STAT_ROWS + whole, PAIR), queries.dtype)]
-        + [jax.ShapeDtypeStruct((2, whole, PAIR), queries.dtype)] * (CHIPS - 1),
+        for t, out in enumerate(outs):
+            j = chunk_ref[2 * t]
+            cols = pl.ds(pl.multiple_of(j * PAIR, PAIR), PAIR)
+            out[pl.ds(0, rows), :] = q_ref[:, cols]
+            if t:
+                out[pl.ds(rows, rows), :] = o_ref[:, cols]
+            at = 2 * rows if t else rows
+            out[pl.ds(at, 2 * rows), :] = x_ref[t, pl.ds(0, 2 * rows), :]
+            both = s_ref[j].astype(jnp.float32) + x_ref[t, pl.ds(2 * rows, STAT_ROWS), :].astype(jnp.float32)
+            out[pl.ds(at + 2 * rows, STAT_ROWS), :] = both.astype(out.dtype)
+
+    return pl.pallas_call(
+        kernel,
+        out_shape=[
+            jax.ShapeDtypeStruct(((4 if t else 3) * rows + STAT_ROWS, PAIR), queries.dtype) for t in range(CHIPS)
+        ],
         in_specs=[SMEM] + [VMEM] * 4,
         out_specs=[VMEM] * CHIPS,
         name="pack_q",
@@ -122,16 +132,23 @@
 
 
 def pack_dq(own, from_sibling):
+    rows = own.shape[1]
+    kept = rows - rows // 4
+
     def kernel(own_ref, x_ref, *outs):
-        for t, out in enumerate(outs):
-            out[0] = own_ref[t]
-            out[1] = x_ref[t]
-
-    return pl.pallas_call(
-        kernel,
-        out_shape=[jax.ShapeDtypeStruct((2,) + own.shape[1:], own.dtype)] * CHIPS,
+        outs[0][pl.ds(0, kept), :] = own_ref[0, pl.ds(0, kept), :]
+        outs[0][pl.ds(kept, rows), :] = x_ref[0]
+        for t in range(1, CHIPS):
+            outs[t][0] = own_ref[t]
+            outs[t][1] = x_ref[t]
+
+    return pl.pallas_call(
+        kernel,
+        out_shape=[jax.ShapeDtypeStruct((kept + rows, PAIR), own.dtype)]
+        + [jax.ShapeDtypeStruct((2,) + own.shape[1:], own.dtype)] * (CHIPS - 1),
         in_specs=[VMEM] * 2,
         out_specs=[VMEM] * CHIPS,
+        cost_estimate=pl.CostEstimate(flops=40 * 10**9, bytes_accessed=2**20, transcendentals=0),
         name="pack_dq",
     )(own, from_sibling)
 
@@ -145,14 +162,11 @@
 
     def kernel(kv_ref, kcol_ref, qrow_ref, slice_ref, *rest):
         ins, rest = rest[:CHIPS], rest[CHIPS:]
-        from_start = (0, rows, 2 * rows)
-        blocks = [(ins[a // 2].at[a % 2], from_start) for a in range(2, N_INNER)]
-        after = rows + STAT_ROWS
-        blocks = [(ins[0], (0, None, rows)), (ins[0], tuple(after + r for r in from_start))] + blocks
+        blocks = [(0, None), (rows, 2 * rows)] + [(0, rows), (2 * rows, 3 * rows)] * (CHIPS - 1)
         dqs = [rest[a % 2].at[a // 2] for a in range(N_INNER)]
-        dkv_ref, q_s, o_s, k_s, v_s, l_s, d_s, dk_s, dv_s = rest[2:]
+        slice_dq, dkv_ref, q_s, o_s, k_s, v_s, l_s, d_s, dk_s, dv_s = rest[2:]
         for a in range(N_INNER):
-            ref, (q_at, o_at, s_at) = blocks[a]
+            ref, (q_at, o_at) = ins[a // 2], blocks[a]
             for part in range(2):
                 to = pl.ds(part * side + a * half, half)
                 at = part * half
@@ -163,13 +177,14 @@
                     o_s[to, :] = ref[pl.ds(o_at + at, half), :]
                 k_s[to, :] = kv_ref[a, pl.ds(at, half), :]
                 v_s[to, :] = kv_ref[a, pl.ds(rows + at, half), :]
-            st = ref[pl.ds(s_at, STAT_ROWS), :].astype(jnp.float32)
+            st = ref[pl.ds(ref.shape[0] - STAT_ROWS, STAT_ROWS), :].astype(jnp.float32)
+            row = 2 * (a % 2)
             for h in range(2):
                 for part in range(2):
                     lanes = slice(h * WIDTH + part * half, h * WIDTH + (part + 1) * half)
                     to = pl.ds(part * side + a * half, half)
-                    l_s[pl.ds(h, 1), to] = st[0:1, lanes] * LOG2E
-                    d_s[pl.ds(h, 1), to] = st[1:2, lanes]
+                    l_s[pl.ds(h, 1), to] = st[row:row + 1, lanes] * LOG2E
+                    d_s[pl.ds(h, 1), to] = st[row + 1:row + 2, lanes]
         nt = (((1,), (1,)), ((), ()))
         f32 = jnp.float32
         for h in range(2):
@@ -200,6 +215,8 @@
                 per = tile // half
                 for a in range(per):
                     dqs[piece * per + a][pl.ds(part * half, half), head] = dq[a * half:(a + 1) * half]
+                if part and piece == 0:
+                    slice_dq[:, head] = dq[half // 2:half]
                 if step == 0:
                     dv_s[...] = dv
                     dk_s[...] = dk
@@ -215,9 +232,9 @@
     return pl.pallas_call(
         kernel,
         out_shape=[jax.ShapeDtypeStruct((CHIPS, rows, PAIR), jnp.bfloat16)] * 2
-        + [jax.ShapeDtypeStruct(kv.shape, jnp.bfloat16)],
+        + [jax.ShapeDtypeStruct((half // 2, PAIR), jnp.bfloat16), jax.ShapeDtypeStruct(kv.shape, jnp.bfloat16)],
         in_specs=[VMEM] * (4 + CHIPS),
-        out_specs=[VMEM] * 3,
+        out_specs=[VMEM] * 4,
         scratch_shapes=[pltpu.VMEM((2 * side, PAIR), jnp.bfloat16)] * 4
         + [pltpu.VMEM((2, 2 * side), jnp.float32)] * 2
         + [pltpu.VMEM((2 * side, WIDTH), jnp.float32)] * 2,
@@ -226,22 +243,26 @@
     )(kv, kcol, qrow, slice_o, *parts)
 
 
-def unpack_q(chunk, parts):
-    rows = parts[0].shape[1]
-
-    def kernel(chunk_ref, *rest):
+def unpack_q(chunk, slice_dq, parts):
+    rows = parts[1].shape[1]
+    kept = rows - slice_dq.shape[0]
+
+    def kernel(chunk_ref, slice_ref, *rest):
         out = rest[-1]
-        for r in range(N_INNER):
-            cols = pl.ds(pl.multiple_of(chunk_ref[r] * PAIR, PAIR), PAIR)
-            out[:, cols] = rest[r // 2][r % 2].astype(jnp.float32)
+        cols = [pl.ds(pl.multiple_of(chunk_ref[r] * PAIR, PAIR), PAIR) for r in range(N_INNER)]
+        out[pl.ds(0, kept), cols[0]] = rest[0][pl.ds(0, kept), :].astype(jnp.float32)
+        out[pl.ds(kept, rows - kept), cols[0]] = slice_ref[...].astype(jnp.float32)
+        out[:, cols[1]] = rest[0][pl.ds(kept, rows), :].astype(jnp.float32)
+        for r in range(2, N_INNER):
+            out[:, cols[r]] = rest[r // 2][r % 2].astype(jnp.float32)
 
     return pl.pallas_call(
         kernel,
         out_shape=jax.ShapeDtypeStruct((rows, N_INNER * PAIR), jnp.float32),
-        in_specs=[SMEM] + [VMEM] * CHIPS,
+        in_specs=[SMEM] + [VMEM] * (1 + CHIPS),
         out_specs=VMEM,
         name="unpack_q",
-    )(chunk, *parts)
+    )(chunk, slice_dq, *parts)
 
 
 def unpack_kv(dkv):
@@ -274,7 +295,7 @@
     senders = jnp.stack([moved_inner(inner_idx, from_wrap - dz, dc) for dz in TURNS for dc in range(2)])
 
     axes = ("outer", "inner")
-    first_leg, second_leg = long_way(outer_count)
+    first_leg, second_leg = long_way(outer_count, False)
 
     kv = lax.all_to_all(pack_kv(keys, values), "inner", 0, 0, tiled=True)
 
@@ -283,9 +304,10 @@
     slice_o = jnp.where(outer_idx % PLANE == 0, middle, slice_o)
 
     stats = jnp.stack([lse.T.reshape(N_INNER, PAIR), delta.T.reshape(N_INNER, PAIR)], axis=1)
-    stats = jnp.pad(stats, ((0, 0), (0, STAT_ROWS - 2), (0, 0)))
+    own_stats = jnp.pad(stats, ((0, 0), (0, STAT_ROWS - 2), (0, 0)))
+    stats = jnp.pad(stats, ((0, 0), (2, STAT_ROWS - 4), (0, 0)))
     crossed = to_sibling(pack_for_sibling(chunk, queries, grad_out, stats))
-    sent = pack_q(chunk, queries, grad_out, stats, crossed)
+    sent = pack_q(chunk, queries, grad_out, own_stats, crossed)
     slice_o = lax.ppermute(slice_o, axes, send_pairs(outer_count, TURNS[0], False, crossing=False) + second_leg)
     parts = [lax.ppermute(x, axes, send_pairs(outer_count, dz, False)) for dz, x in zip(TURNS, sent)]
 
@@ -295,13 +317,17 @@
     kcol = jnp.repeat(key_c, half)[:, None]
     qrow = jnp.repeat(query_c, half)[None, :]
 
-    own_dq, sibling_dq, dkv = attend(kv, parts, slice_o, kcol, qrow)
+    own_dq, sibling_dq, slice_dq, dkv = attend(kv, parts, slice_o, kcol, qrow)
     dkv = lax.all_to_all(dkv, "inner", 0, 0, tiled=True)
+    first_leg, second_leg = long_way(outer_count, True)
+    middle = lax.ppermute(slice_dq, axes, first_leg)
     sent = pack_dq(own_dq, to_sibling(sibling_dq))
     back = [lax.ppermute(x, axes, send_pairs(outer_count, dz, True)) for dz, x in zip(TURNS, sent)]
+    slice_dq = jnp.where(outer_idx % PLANE == PLANE - 1, middle, slice_dq)
+    slice_dq = lax.ppermute(slice_dq, axes, send_pairs(outer_count, TURNS[0], True, crossing=False) + second_leg)
     grad_k, grad_v = unpack_kv(dkv)
     back, grad_k, grad_v = lax.optimization_barrier((back, grad_k, grad_v))
-    grad_q = unpack_q(chunk, back)
+    grad_q = unpack_q(chunk, slice_dq, back)
     return grad_q, grad_k, grad_v
 
 

time: 220 us -> 219 us (level)
  waiting for transfers between devices: 103 us -> 98.7 us
    ppermute x4, waiting for transfers between devices: 49.8 us -> 20.1 us  [shards(): lax.ppermute(x, axes, send_pairs(outer_count, dz, True))]
    all_to_all x1, waiting for transfers between devices: 0.01 us -> 26.3 us  [shards(): dkv = lax.all_to_all(dkv, 'inner', 0, 0, tiled=True)]
    ppermute x1, waiting for transfers between devices: 37.1 us -> 45.6 us  [shards(): lax.ppermute(slice_o, axes, send_pairs(outer_count, TURNS[0], False, cros...]
    ppermute x1, waiting for transfers between devices: 14.2 us -> 6.71 us  [shards(): middle = lax.ppermute(slice_o, axes, first_leg)]
    ppermute x0 -> x2, starting transfers between devices: none -> 3.56 us  [the longest x1 2.91 us: shards(): lax.ppermute(slice_dq, axes, send_pairs(outer_count, TURNS[0], True, cros...]
    unnamed x22 -> x24, local copies, waits for them, and re-layouts: 5.92 us -> 6.51 us
  transfers between devices with their start and end apart: 14 -> 16, of which waited for: 5 -> 5; matrix products, arithmetic and copies ran while one was open for 2% -> 2% of each run, Pallas kernels for 4% -> 4%
where the time goes in v4:
time: 219 us; the launch traced here: 218 us
  waiting for transfers between devices  98.7 us (45%)
  starting transfers between devices  88.5 us (40%)
  Pallas kernels  18.5 us (8%)
  local copies, waits for them, and re-layouts  10 us (5%)
    ppermute x1, waiting for transfers between devices, shards(): lax.ppermute(slice_o, axes, send_pairs(outer_count, TURNS[0], False, cros...  45.6 us
    all_to_all x1, waiting for transfers between devices, shards(): dkv = lax.all_to_all(dkv, 'inner', 0, 0, tiled=True)  26.3 us
    ppermute x4, starting transfers between devices, shards(): lax.ppermute(x, axes, send_pairs(outer_count, dz, True))  26 us
    ppermute x4, starting transfers between devices, shards(): lax.ppermute(x, axes, send_pairs(outer_count, dz, False))  23 us
    ppermute x4, waiting for transfers between devices, shards(): lax.ppermute(x, axes, send_pairs(outer_count, dz, True))  20.1 us
    all_to_all x1, starting transfers between devices, shards(): kv = lax.all_to_all(pack_kv(keys, values), 'inner', 0, 0, tiled=True)  14.9 us
    all_to_all x1, starting transfers between devices, shards(): dkv = lax.all_to_all(dkv, 'inner', 0, 0, tiled=True)  7.59 us
    ppermute x1, waiting for transfers between devices, shards(): middle = lax.ppermute(slice_o, axes, first_leg)  6.71 us
  transfers between devices with their start and end apart: 16, of which 5 were waited for; matrix products, arithmetic and copies ran while one was open for 2% of the time, Pallas kernels for 4%

profile of v4, /device:TPU:33, one launch (start us, length us, event | category | flops | bytes accessed | tf_op | source)
XLA Modules:
  0.0 217.6 jit_solution(15846899656910563558)
XLA Ops:
  0.6 2.2 %pack_kv.1 = bf16[8,256,256]{2,1,0:T(8,128)(2,1)} custom-call(bf16[128,2048]{1,0:T(8,128)(2,1)} %k_ref.1, bf16[128,2048]{1,0:T(8,128)(2,1)} %v_ref.1), custom_call_target="tpu_custom_call" | custom-call | tf_op jit(solution)/shard_map/pack_kv/pallas_call | solution.py:75
  2.9 14.9 %all-to-all-start = ((bf16[8,256,256]{2,1,0:T(8,128)(2,1)}), bf16[8,256,256]{2,1,0:T(8,128)(2,1)S(1)}, u32[]{:S(2)}, u32[]{:S(2)}) async-start(bf16[8,256,256]{2,1,0:T(8,128)(2,1)} %pack_kv.1), calls=%async_computation | async-start | bytes 2097152 | tf_op jit(solution)/shard_map/all_to_all | solution.py:300
  17.7 0.7 copy-done.8
  18.4 0.7 copy-done.9
  19.1 0.7 stack.65.chunk_ref
  19.8 0.7 fusion.3
  20.5 2.1 pack_for_sibling.1
  22.6 1.9 collective-permute-start.2
  24.5 0.8 constant_dynamic-slice_fusion
  25.4 6.7 %collective-permute-start = (bf16[128,256]{1,0:T(8,128)(2,1)S(1)}, bf16[128,256]{1,0:T(8,128)(2,1)S(1)}, u32[]{:S(2)}, u32[]{:S(2)}) collective-permute-start(bf16[128,256]{1,0:T(8,128)(2,1)S(1)} %constant_dynamic-slice_fusion), channel_id=1, source_target_pairs={{0,262},{1,263},{2,256},{3,257},{4,258},{5,259},{6,260},{7,261},{1... | collective-permute-start | bytes 196616 | tf_op jit(solution)/shard_map/ppermute | solution.py:303
  32.1 0.7 copy-done.10
  32.8 0.1 reshape_squeeze.3
  32.9 0.1 stack.74
  33.1 0.8 copy-done.2
  33.9 2.4 %pack_q.1 = (bf16[400,256]{1,0:T(8,128)(2,1)}, bf16[528,256]{1,0:T(8,128)(2,1)}, bf16[528,256]{1,0:T(8,128)(2,1)}, bf16[528,256]{1,0:T(8,128)(2,1)}) custom-call(s32[8]{0:T(128)} %stack.65.chunk_ref, bf16[128,2048]{1,0:T(8,128)(2,1)} %q_ref.3, bf16[128,2048]{1,0:T(8,128)(2,1)} %o_ref.3, bf16[8,16,256]{2,1,0:T(8,128)(2,1)} %get-tuple-element.46.s_ref, ...), custom_call_target="tpu_custom_call" | custom-call | tf_op jit(solution)/shard_map/pack_q/pallas_call | solution.py:123
  36.3 10.5 %collective-permute-start.3 = (bf16[400,256]{1,0:T(8,128)(2,1)}, bf16[400,256]{1,0:T(8,128)(2,1)S(1)}, u32[]{:S(2)}, u32[]{:S(2)}) collective-permute-start(bf16[400,256]{1,0:T(8,128)(2,1)} %get-tuple-element.23), channel_id=1, source_target_pairs={{0,506},{1,507},{2,508},{3,509},{4,510},{5,511},{6,504},{7,505},{8... | collective-permute-start | bytes 614408 | tf_op jit(solution)/shard_map/ppermute | solution.py:312
  46.8 2.5 %collective-permute-start.4 = (bf16[528,256]{1,0:T(8,128)(2,1)}, bf16[528,256]{1,0:T(8,128)(2,1)S(1)}, u32[]{:S(2)}, u32[]{:S(2)}) collective-permute-start(bf16[528,256]{1,0:T(8,128)(2,1)} %get-tuple-element.24), channel_id=1, source_target_pairs={{0,504},{1,505},{2,506},{3,507},{4,508},{5,509},{6,510},{7,511},{8... | collective-permute-start | bytes 811016 | tf_op jit(solution)/shard_map/ppermute | solution.py:312
  49.3 7.9 %collective-permute-start.5 = (bf16[528,256]{1,0:T(8,128)(2,1)}, bf16[528,256]{1,0:T(8,128)(2,1)S(1)}, u32[]{:S(2)}, u32[]{:S(2)}) collective-permute-start(bf16[528,256]{1,0:T(8,128)(2,1)} %get-tuple-element.25), channel_id=1, source_target_pairs={{0,508},{1,509},{2,510},{3,511},{4,504},{5,505},{6,506},{7,507},{8... | collective-permute-start | bytes 811016 | tf_op jit(solution)/shard_map/ppermute | solution.py:312
  57.1 2.2 collective-permute-start.6
  59.3 6.7 %collective-permute-done = bf16[128,256]{1,0:T(8,128)(2,1)S(1)} collective-permute-done((bf16[128,256]{1,0:T(8,128)(2,1)S(1)}, bf16[128,256]{1,0:T(8,128)(2,1)S(1)}, u32[]{:S(2)}, u32[]{:S(2)}) %collective-permute-start) | collective-permute-done | bytes 65568 | tf_op jit(solution)/shard_map/ppermute | solution.py:303
  66.0 0.9 broadcast_select_fusion
  66.9 1.9 collective-permute-start.1
  68.8 0.6 gather_fusion
  69.5 0.1 broadcast_in_dim.8
  69.5 0.1 broadcast_in_dim_reshape.7.qrow_ref
  69.6 0.1 broadcast_in_dim.7
  69.7 0.2 broadcast_in_dim_reshape.8.kcol_ref
  69.9 45.6 %collective-permute-done.1.slice_ref = bf16[128,256]{1,0:T(8,128)(2,1)S(1)} collective-permute-done((bf16[128,256]{1,0:T(8,128)(2,1)S(1)}, bf16[128,256]{1,0:T(8,128)(2,1)S(1)}, u32[]{:S(2)}, u32[]{:S(2)}) %collective-permute-start.1) | collective-permute-done | bytes 65568 | tf_op jit(solution)/shard_map/ppermute | solution.py:311
  115.5 5.1 %attend.1 = (bf16[4,128,256]{2,1,0:T(8,128)(2,1)S(1)}, bf16[4,128,256]{2,1,0:T(8,128)(2,1)S(1)}, bf16[32,256]{1,0:T(8,128)(2,1)S(1)}, bf16[8,256,256]{2,1,0:T(8,128)(2,1)}) custom-call(bf16[8,256,256]{2,1,0:T(8,128)(2,1)S(1)} %all-to-all-done.kv_ref, s32[512,1]{1,0:T(8,128)S(1)} %broadcast_in_dim_reshape.8.kcol_ref, ...), custom_call_target="tpu_custom_call" | custom-call | tf_op jit(solution)/shard_map/attend/pallas_call | solution.py:232
  120.6 0.7 copy-done
  121.3 3.0 %collective-permute-start.9 = (bf16[4,128,256]{2,1,0:T(8,128)(2,1)S(1)}, bf16[4,128,256]{2,1,0:T(8,128)(2,1)S(1)}, u32[]{:S(2)}, u32[]{:S(2)}) collective-permute-start(bf16[4,128,256]{2,1,0:T(8,128)(2,1)S(1)} %get-tuple-element.29), channel_id=1, source_target_pairs={{0,1},{1,0},{2,3},{3,2},{4,5},{5,4},{6,7},{7,6},{8,9},{9,8},{10,11... | collective-permute-start | bytes 786440 | tf_op jit(solution)/shard_map/ppermute | solution.py:59
  124.3 7.6 %all-to-all-start.1 = ((bf16[8,256,256]{2,1,0:T(8,128)(2,1)}), bf16[8,256,256]{2,1,0:T(8,128)(2,1)S(1)}, u32[]{:S(2)}, u32[]{:S(2)}) async-start(bf16[8,256,256]{2,1,0:T(8,128)(2,1)} %get-tuple-element.34), calls=%async_computation.1 | async-start | bytes 2097152 | tf_op jit(solution)/shard_map/all_to_all | solution.py:321
  131.9 0.7 collective-permute-start.7
  132.6 0.7 copy-done.11
  133.3 1.8 pack_dq.1
  135.1 12.0 %collective-permute-start.10 = (bf16[224,256]{1,0:T(8,128)(2,1)}, bf16[224,256]{1,0:T(8,128)(2,1)S(1)}, u32[]{:S(2)}, u32[]{:S(2)}) collective-permute-start(bf16[224,256]{1,0:T(8,128)(2,1)} %get-tuple-element.30), channel_id=1, source_target_pairs={{506,0},{507,1},{508,2},{509,3},{510,4},{511,5},{504,6},{505,7},{4... | collective-permute-start | bytes 344072 | tf_op jit(solution)/shard_map/ppermute | solution.py:325
  147.2 2.9 %collective-permute-start.11 = (bf16[2,128,256]{2,1,0:T(8,128)(2,1)}, bf16[2,128,256]{2,1,0:T(8,128)(2,1)S(1)}, u32[]{:S(2)}, u32[]{:S(2)}) collective-permute-start(bf16[2,128,256]{2,1,0:T(8,128)(2,1)} %get-tuple-element.31), channel_id=1, source_target_pairs={{504,0},{505,1},{506,2},{507,3},{508,4},{509,5},{510,6},{511,7},{2... | collective-permute-start | bytes 393224 | tf_op jit(solution)/shard_map/ppermute | solution.py:325
  150.1 8.9 %collective-permute-start.12 = (bf16[2,128,256]{2,1,0:T(8,128)(2,1)}, bf16[2,128,256]{2,1,0:T(8,128)(2,1)S(1)}, u32[]{:S(2)}, u32[]{:S(2)}) collective-permute-start(bf16[2,128,256]{2,1,0:T(8,128)(2,1)} %get-tuple-element.32), channel_id=1, source_target_pairs={{508,0},{509,1},{510,2},{511,3},{504,4},{505,5},{506,6},{507,7},{6... | collective-permute-start | bytes 393224 | tf_op jit(solution)/shard_map/ppermute | solution.py:325
  159.0 2.1 collective-permute-start.13
  161.2 2.9 %collective-permute-start.8 = (bf16[32,256]{1,0:T(8,128)(2,1)S(1)}, bf16[32,256]{1,0:T(8,128)(2,1)S(1)}, u32[]{:S(2)}, u32[]{:S(2)}) collective-permute-start(bf16[32,256]{1,0:T(8,128)(2,1)S(1)} %broadcast_select_fusion.1), channel_id=1, source_target_pairs={{4,8},{5,9},{6,10},{7,11},{0,12},{1,13},{2,14},{3,15},{12,16},{13,... | collective-permute-start | bytes 49160 | tf_op jit(solution)/shard_map/ppermute | solution.py:327
  164.1 26.3 %all-to-all-done.1.in_ref = bf16[8,256,256]{2,1,0:T(8,128)(2,1)S(1)} async-done(((bf16[8,256,256]{2,1,0:T(8,128)(2,1)}), bf16[8,256,256]{2,1,0:T(8,128)(2,1)S(1)}, u32[]{:S(2)}, u32[]{:S(2)}) %all-to-all-start.1) | async-done | bytes 1048608 | tf_op jit(solution)/shard_map/all_to_all | solution.py:321
  190.4 1.0 copy-done.1
  191.4 2.7 %unpack_kv.1 = (f32[128,2048]{1,0:T(8,128)}, f32[128,2048]{1,0:T(8,128)}) custom-call(bf16[8,256,256]{2,1,0:T(8,128)(2,1)} %copy-done.1), custom_call_target="tpu_custom_call" | custom-call | tf_op jit(solution)/shard_map/unpack_kv/pallas_call | solution.py:277
  194.1 14.9 %collective-permute-done.10.rest_0_ = bf16[224,256]{1,0:T(8,128)(2,1)S(1)} collective-permute-done((bf16[224,256]{1,0:T(8,128)(2,1)}, bf16[224,256]{1,0:T(8,128)(2,1)S(1)}, u32[]{:S(2)}, u32[]{:S(2)}) %collective-permute-start.10) | collective-permute-done | bytes 114720 | tf_op jit(solution)/shard_map/ppermute | solution.py:325
  209.0 5.1 %collective-permute-done.11.rest_1_ = bf16[2,128,256]{2,1,0:T(8,128)(2,1)S(1)} collective-permute-done((bf16[2,128,256]{2,1,0:T(8,128)(2,1)}, bf16[2,128,256]{2,1,0:T(8,128)(2,1)S(1)}, u32[]{:S(2)}, u32[]{:S(2)}) %collective-permute-start.11) | collective-permute-done | bytes 131104 | tf_op jit(solution)/shard_map/ppermute | solution.py:325
  214.2 0.6 copy-done.3
  214.9 0.6 copy-done.7
  215.5 2.2 unpack_q.1
  (34 shorter events, 0.2 us)
Async XLA Ops:
  2.9 112.6 %all-to-all-start = ((bf16[8,256,256]{2,1,0:T(8,128)(2,1)}), bf16[8,256,256]{2,1,0:T(8,128)(2,1)S(1)}, u32[]{:S(2)}, u32[]{:S(2)}) async-start(bf16[8,256,256]{2,1,0:T(8,128)(2,1)} %pack_kv.1), calls=%async_computation | async-start | bytes 2097152 | tf_op jit(solution)/shard_map/all_to_all | solution.py:300
  17.7 0.7 copy-start.8
  18.4 0.7 copy-start.9
  22.6 10.5 %collective-permute-start.2 = (bf16[4,272,256]{2,1,0:T(8,128)(2,1)}, bf16[4,272,256]{2,1,0:T(8,128)(2,1)S(1)}, u32[]{:S(2)}, u32[]{:S(2)}) collective-permute-start(bf16[4,272,256]{2,1,0:T(8,128)(2,1)} %pack_for_sibling.1), channel_id=1, source_target_pairs={{0,1},{1,0},{2,3},{3,2},{4,5},{5,4},{6,7},{7,6},{8,9},{9,8},{10,11... | collective-permute-start | bytes 1671176 | tf_op jit(solution)/shard_map/ppermute | solution.py:59
  25.4 40.7 %collective-permute-start = (bf16[128,256]{1,0:T(8,128)(2,1)S(1)}, bf16[128,256]{1,0:T(8,128)(2,1)S(1)}, u32[]{:S(2)}, u32[]{:S(2)}) collective-permute-start(bf16[128,256]{1,0:T(8,128)(2,1)S(1)} %constant_dynamic-slice_fusion), channel_id=1, source_target_pairs={{0,262},{1,263},{2,256},{3,257},{4,258},{5,259},{6,260},{7,261},{1... | collective-permute-start | bytes 196616 | tf_op jit(solution)/shard_map/ppermute | solution.py:303
  32.1 0.7 copy-start.10
  33.1 0.8 copy-start.2
  36.3 79.2 %collective-permute-start.3 = (bf16[400,256]{1,0:T(8,128)(2,1)}, bf16[400,256]{1,0:T(8,128)(2,1)S(1)}, u32[]{:S(2)}, u32[]{:S(2)}) collective-permute-start(bf16[400,256]{1,0:T(8,128)(2,1)} %get-tuple-element.23), channel_id=1, source_target_pairs={{0,506},{1,507},{2,508},{3,509},{4,510},{5,511},{6,504},{7,505},{8... | collective-permute-start | bytes 614408 | tf_op jit(solution)/shard_map/ppermute | solution.py:312
  46.8 68.7 %collective-permute-start.4 = (bf16[528,256]{1,0:T(8,128)(2,1)}, bf16[528,256]{1,0:T(8,128)(2,1)S(1)}, u32[]{:S(2)}, u32[]{:S(2)}) collective-permute-start(bf16[528,256]{1,0:T(8,128)(2,1)} %get-tuple-element.24), channel_id=1, source_target_pairs={{0,504},{1,505},{2,506},{3,507},{4,508},{5,509},{6,510},{7,511},{8... | collective-permute-start | bytes 811016 | tf_op jit(solution)/shard_map/ppermute | solution.py:312
  49.3 66.2 %collective-permute-start.5 = (bf16[528,256]{1,0:T(8,128)(2,1)}, bf16[528,256]{1,0:T(8,128)(2,1)S(1)}, u32[]{:S(2)}, u32[]{:S(2)}) collective-permute-start(bf16[528,256]{1,0:T(8,128)(2,1)} %get-tuple-element.25), channel_id=1, source_target_pairs={{0,508},{1,509},{2,510},{3,511},{4,504},{5,505},{6,506},{7,507},{8... | collective-permute-start | bytes 811016 | tf_op jit(solution)/shard_map/ppermute | solution.py:312
  57.1 58.4 %collective-permute-start.6 = (bf16[528,256]{1,0:T(8,128)(2,1)}, bf16[528,256]{1,0:T(8,128)(2,1)S(1)}, u32[]{:S(2)}, u32[]{:S(2)}) collective-permute-start(bf16[528,256]{1,0:T(8,128)(2,1)} %get-tuple-element.26), channel_id=1, source_target_pairs={{0,510},{1,511},{2,504},{3,505},{4,506},{5,507},{6,508},{7,509},{8... | collective-permute-start | bytes 811016 | tf_op jit(solution)/shard_map/ppermute | solution.py:312
  66.9 48.6 %collective-permute-start.1 = (bf16[128,256]{1,0:T(8,128)(2,1)S(1)}, bf16[128,256]{1,0:T(8,128)(2,1)S(1)}, u32[]{:S(2)}, u32[]{:S(2)}) collective-permute-start(bf16[128,256]{1,0:T(8,128)(2,1)S(1)} %broadcast_select_fusion), channel_id=1, source_target_pairs={{8,4},{9,5},{10,6},{11,7},{12,0},{13,1},{14,2},{15,3},{16,12},{17,... | collective-permute-start | bytes 196616 | tf_op jit(solution)/shard_map/ppermute | solution.py:311
  120.6 0.7 copy-start
  121.3 11.2 %collective-permute-start.9 = (bf16[4,128,256]{2,1,0:T(8,128)(2,1)S(1)}, bf16[4,128,256]{2,1,0:T(8,128)(2,1)S(1)}, u32[]{:S(2)}, u32[]{:S(2)}) collective-permute-start(bf16[4,128,256]{2,1,0:T(8,128)(2,1)S(1)} %get-tuple-element.29), channel_id=1, source_target_pairs={{0,1},{1,0},{2,3},{3,2},{4,5},{5,4},{6,7},{7,6},{8,9},{9,8},{10,11... | collective-permute-start | bytes 786440 | tf_op jit(solution)/shard_map/ppermute | solution.py:59
  124.3 66.1 %all-to-all-start.1 = ((bf16[8,256,256]{2,1,0:T(8,128)(2,1)}), bf16[8,256,256]{2,1,0:T(8,128)(2,1)S(1)}, u32[]{:S(2)}, u32[]{:S(2)}) async-start(bf16[8,256,256]{2,1,0:T(8,128)(2,1)} %get-tuple-element.34), calls=%async_computation.1 | async-start | bytes 2097152 | tf_op jit(solution)/shard_map/all_to_all | solution.py:321
  131.9 29.2 %collective-permute-start.7 = (bf16[32,256]{1,0:T(8,128)(2,1)S(1)}, bf16[32,256]{1,0:T(8,128)(2,1)S(1)}, u32[]{:S(2)}, u32[]{:S(2)}) collective-permute-start(bf16[32,256]{1,0:T(8,128)(2,1)S(1)} %get-tuple-element.27), channel_id=1, source_target_pairs={{506,252},{507,253},{508,254},{509,255},{510,248},{511,249},{504,2... | collective-permute-start | bytes 49160 | tf_op jit(solution)/shard_map/ppermute | solution.py:323
  132.6 0.7 copy-start.11
  135.1 73.9 %collective-permute-start.10 = (bf16[224,256]{1,0:T(8,128)(2,1)}, bf16[224,256]{1,0:T(8,128)(2,1)S(1)}, u32[]{:S(2)}, u32[]{:S(2)}) collective-permute-start(bf16[224,256]{1,0:T(8,128)(2,1)} %get-tuple-element.30), channel_id=1, source_target_pairs={{506,0},{507,1},{508,2},{509,3},{510,4},{511,5},{504,6},{505,7},{4... | collective-permute-start | bytes 344072 | tf_op jit(solution)/shard_map/ppermute | solution.py:325
  147.2 67.0 %collective-permute-start.11 = (bf16[2,128,256]{2,1,0:T(8,128)(2,1)}, bf16[2,128,256]{2,1,0:T(8,128)(2,1)S(1)}, u32[]{:S(2)}, u32[]{:S(2)}) collective-permute-start(bf16[2,128,256]{2,1,0:T(8,128)(2,1)} %get-tuple-element.31), channel_id=1, source_target_pairs={{504,0},{505,1},{506,2},{507,3},{508,4},{509,5},{510,6},{511,7},{2... | collective-permute-start | bytes 393224 | tf_op jit(solution)/shard_map/ppermute | solution.py:325
  150.1 64.0 %collective-permute-start.12 = (bf16[2,128,256]{2,1,0:T(8,128)(2,1)}, bf16[2,128,256]{2,1,0:T(8,128)(2,1)S(1)}, u32[]{:S(2)}, u32[]{:S(2)}) collective-permute-start(bf16[2,128,256]{2,1,0:T(8,128)(2,1)} %get-tuple-element.32), channel_id=1, source_target_pairs={{508,0},{509,1},{510,2},{511,3},{504,4},{505,5},{506,6},{507,7},{6... | collective-permute-start | bytes 393224 | tf_op jit(solution)/shard_map/ppermute | solution.py:325
  159.0 55.1 %collective-permute-start.13 = (bf16[2,128,256]{2,1,0:T(8,128)(2,1)}, bf16[2,128,256]{2,1,0:T(8,128)(2,1)S(1)}, u32[]{:S(2)}, u32[]{:S(2)}) collective-permute-start(bf16[2,128,256]{2,1,0:T(8,128)(2,1)} %get-tuple-element.33), channel_id=1, source_target_pairs={{510,0},{511,1},{504,2},{505,3},{506,4},{507,5},{508,6},{509,7},{0... | collective-permute-start | bytes 393224 | tf_op jit(solution)/shard_map/ppermute | solution.py:325
  161.2 53.0 %collective-permute-start.8 = (bf16[32,256]{1,0:T(8,128)(2,1)S(1)}, bf16[32,256]{1,0:T(8,128)(2,1)S(1)}, u32[]{:S(2)}, u32[]{:S(2)}) collective-permute-start(bf16[32,256]{1,0:T(8,128)(2,1)S(1)} %broadcast_select_fusion.1), channel_id=1, source_target_pairs={{4,8},{5,9},{6,10},{7,11},{0,12},{1,13},{2,14},{3,15},{12,16},{13,... | collective-permute-start | bytes 49160 | tf_op jit(solution)/shard_map/ppermute | solution.py:327
  190.4 1.0 copy-start.1
  209.0 5.2 %copy-start.6 = (bf16[224,256]{1,0:T(8,128)(2,1)}, bf16[224,256]{1,0:T(8,128)(2,1)S(1)}, u32[]{:S(2)}) copy-start(bf16[224,256]{1,0:T(8,128)(2,1)S(1)} %collective-permute-done.10.rest_0_) | copy-start | bytes 344068
  214.1 0.7 copy-start.3
  214.1 0.7 copy-start.4
  214.1 0.7 copy-start.5
  214.9 0.6 copy-start.7

commit v5 on v4

--- a/solution.py
+++ b/solution.py
@@ -148,7 +148,7 @@
         + [jax.ShapeDtypeStruct((2,) + own.shape[1:], own.dtype)] * (CHIPS - 1),
         in_specs=[VMEM] * 2,
         out_specs=[VMEM] * CHIPS,
-        cost_estimate=pl.CostEstimate(flops=40 * 10**9, bytes_accessed=2**20, transcendentals=0),
+        cost_estimate=pl.CostEstimate(flops=4 * 10**9, bytes_accessed=2**20, transcendentals=0),
         name="pack_dq",
     )(own, from_sibling)
 

time: 219 us -> 216 us (0.986)
  waiting for transfers between devices: 98.7 us -> 96.4 us
    all_to_all x1, waiting for transfers between devices: 26.3 us -> 23.6 us  [shards(): dkv = lax.all_to_all(dkv, 'inner', 0, 0, tiled=True)]
  transfers between devices with their start and end apart: 16 -> 16, of which waited for: 5 -> 6; matrix products, arithmetic and copies ran while one was open for 2% -> 2% of each run, Pallas kernels for 4% -> 4%
where the time goes in v5:
time: 216 us; the launch traced here: 215 us
  waiting for transfers between devices  96.4 us (45%)
  starting transfers between devices  88.4 us (41%)
  Pallas kernels  18.5 us (9%)
  local copies, waits for them, and re-layouts  10 us (5%)
    ppermute x1, waiting for transfers between devices, shards(): lax.ppermute(slice_o, axes, send_pairs(outer_count, TURNS[0], False, cros...  45.6 us
    ppermute x4, starting transfers between devices, shards(): lax.ppermute(x, axes, send_pairs(outer_count, dz, True))  26 us
    all_to_all x1, waiting for transfers between devices, shards(): dkv = lax.all_to_all(dkv, 'inner', 0, 0, tiled=True)  23.6 us
    ppermute x4, starting transfers between devices, shards(): lax.ppermute(x, axes, send_pairs(outer_count, dz, False))  23 us
    ppermute x4, waiting for transfers between devices, shards(): lax.ppermute(x, axes, send_pairs(outer_count, dz, True))  19.7 us
    all_to_all x1, starting transfers between devices, shards(): kv = lax.all_to_all(pack_kv(keys, values), 'inner', 0, 0, tiled=True)  14.9 us
    all_to_all x1, starting transfers between devices, shards(): dkv = lax.all_to_all(dkv, 'inner', 0, 0, tiled=True)  8.55 us
    ppermute x1, waiting for transfers between devices, shards(): middle = lax.ppermute(slice_o, axes, first_leg)  6.71 us
  transfers between devices with their start and end apart: 16, of which 6 were waited for; matrix products, arithmetic and copies ran while one was open for 2% of the time, Pallas kernels for 4%

profile of v5, /device:TPU:33, one launch (start us, length us, event | category | flops | bytes accessed | tf_op | source)
XLA Modules:
  0.0 215.2 jit_solution(17590352975740773668)
XLA Ops:
  0.6 2.2 %pack_kv.1 = bf16[8,256,256]{2,1,0:T(8,128)(2,1)} custom-call(bf16[128,2048]{1,0:T(8,128)(2,1)} %k_ref.1, bf16[128,2048]{1,0:T(8,128)(2,1)} %v_ref.1), custom_call_target="tpu_custom_call" | custom-call | tf_op jit(solution)/shard_map/pack_kv/pallas_call | solution.py:75
  2.9 14.9 %all-to-all-start = ((bf16[8,256,256]{2,1,0:T(8,128)(2,1)}), bf16[8,256,256]{2,1,0:T(8,128)(2,1)S(1)}, u32[]{:S(2)}, u32[]{:S(2)}) async-start(bf16[8,256,256]{2,1,0:T(8,128)(2,1)} %pack_kv.1), calls=%async_computation | async-start | bytes 2097152 | tf_op jit(solution)/shard_map/all_to_all | solution.py:300
  17.7 0.7 copy-done.8
  18.4 0.7 copy-done.9
  19.1 0.7 stack.65.chunk_ref
  19.8 0.7 fusion.3
  20.5 2.1 pack_for_sibling.1
  22.6 1.9 collective-permute-start.2
  24.5 0.8 constant_dynamic-slice_fusion
  25.4 6.7 %collective-permute-start = (bf16[128,256]{1,0:T(8,128)(2,1)S(1)}, bf16[128,256]{1,0:T(8,128)(2,1)S(1)}, u32[]{:S(2)}, u32[]{:S(2)}) collective-permute-start(bf16[128,256]{1,0:T(8,128)(2,1)S(1)} %constant_dynamic-slice_fusion), channel_id=1, source_target_pairs={{0,262},{1,263},{2,256},{3,257},{4,258},{5,259},{6,260},{7,261},{1... | collective-permute-start | bytes 196616 | tf_op jit(solution)/shard_map/ppermute | solution.py:303
  32.1 0.7 copy-done.10
  32.8 0.1 reshape_squeeze.3
  32.9 0.1 stack.74
  33.1 0.8 copy-done.2
  33.9 2.4 %pack_q.1 = (bf16[400,256]{1,0:T(8,128)(2,1)}, bf16[528,256]{1,0:T(8,128)(2,1)}, bf16[528,256]{1,0:T(8,128)(2,1)}, bf16[528,256]{1,0:T(8,128)(2,1)}) custom-call(s32[8]{0:T(128)} %stack.65.chunk_ref, bf16[128,2048]{1,0:T(8,128)(2,1)} %q_ref.3, bf16[128,2048]{1,0:T(8,128)(2,1)} %o_ref.3, bf16[8,16,256]{2,1,0:T(8,128)(2,1)} %get-tuple-element.46.s_ref, ...), custom_call_target="tpu_custom_call" | custom-call | tf_op jit(solution)/shard_map/pack_q/pallas_call | solution.py:123
  36.3 10.5 %collective-permute-start.3 = (bf16[400,256]{1,0:T(8,128)(2,1)}, bf16[400,256]{1,0:T(8,128)(2,1)S(1)}, u32[]{:S(2)}, u32[]{:S(2)}) collective-permute-start(bf16[400,256]{1,0:T(8,128)(2,1)} %get-tuple-element.23), channel_id=1, source_target_pairs={{0,506},{1,507},{2,508},{3,509},{4,510},{5,511},{6,504},{7,505},{8... | collective-permute-start | bytes 614408 | tf_op jit(solution)/shard_map/ppermute | solution.py:312
  46.8 2.5 %collective-permute-start.4 = (bf16[528,256]{1,0:T(8,128)(2,1)}, bf16[528,256]{1,0:T(8,128)(2,1)S(1)}, u32[]{:S(2)}, u32[]{:S(2)}) collective-permute-start(bf16[528,256]{1,0:T(8,128)(2,1)} %get-tuple-element.24), channel_id=1, source_target_pairs={{0,504},{1,505},{2,506},{3,507},{4,508},{5,509},{6,510},{7,511},{8... | collective-permute-start | bytes 811016 | tf_op jit(solution)/shard_map/ppermute | solution.py:312
  49.3 7.9 %collective-permute-start.5 = (bf16[528,256]{1,0:T(8,128)(2,1)}, bf16[528,256]{1,0:T(8,128)(2,1)S(1)}, u32[]{:S(2)}, u32[]{:S(2)}) collective-permute-start(bf16[528,256]{1,0:T(8,128)(2,1)} %get-tuple-element.25), channel_id=1, source_target_pairs={{0,508},{1,509},{2,510},{3,511},{4,504},{5,505},{6,506},{7,507},{8... | collective-permute-start | bytes 811016 | tf_op jit(solution)/shard_map/ppermute | solution.py:312
  57.1 2.2 %collective-permute-start.6 = (bf16[528,256]{1,0:T(8,128)(2,1)}, bf16[528,256]{1,0:T(8,128)(2,1)S(1)}, u32[]{:S(2)}, u32[]{:S(2)}) collective-permute-start(bf16[528,256]{1,0:T(8,128)(2,1)} %get-tuple-element.26), channel_id=1, source_target_pairs={{0,510},{1,511},{2,504},{3,505},{4,506},{5,507},{6,508},{7,509},{8... | collective-permute-start | bytes 811016 | tf_op jit(solution)/shard_map/ppermute | solution.py:312
  59.3 6.7 %collective-permute-done = bf16[128,256]{1,0:T(8,128)(2,1)S(1)} collective-permute-done((bf16[128,256]{1,0:T(8,128)(2,1)S(1)}, bf16[128,256]{1,0:T(8,128)(2,1)S(1)}, u32[]{:S(2)}, u32[]{:S(2)}) %collective-permute-start) | collective-permute-done | bytes 65568 | tf_op jit(solution)/shard_map/ppermute | solution.py:303
  66.0 0.9 broadcast_select_fusion
  66.9 1.9 collective-permute-start.1
  68.8 0.6 gather_fusion
  69.5 0.1 broadcast_in_dim.8
  69.5 0.1 broadcast_in_dim_reshape.7.qrow_ref
  69.7 0.2 broadcast_in_dim_reshape.8.kcol_ref
  69.9 45.6 %collective-permute-done.1.slice_ref = bf16[128,256]{1,0:T(8,128)(2,1)S(1)} collective-permute-done((bf16[128,256]{1,0:T(8,128)(2,1)S(1)}, bf16[128,256]{1,0:T(8,128)(2,1)S(1)}, u32[]{:S(2)}, u32[]{:S(2)}) %collective-permute-start.1) | collective-permute-done | bytes 65568 | tf_op jit(solution)/shard_map/ppermute | solution.py:311
  115.5 5.1 %attend.1 = (bf16[4,128,256]{2,1,0:T(8,128)(2,1)S(1)}, bf16[4,128,256]{2,1,0:T(8,128)(2,1)S(1)}, bf16[32,256]{1,0:T(8,128)(2,1)S(1)}, bf16[8,256,256]{2,1,0:T(8,128)(2,1)}) custom-call(bf16[8,256,256]{2,1,0:T(8,128)(2,1)S(1)} %all-to-all-done.kv_ref, s32[512,1]{1,0:T(8,128)S(1)} %broadcast_in_dim_reshape.8.kcol_ref, ...), custom_call_target="tpu_custom_call" | custom-call | tf_op jit(solution)/shard_map/attend/pallas_call | solution.py:232
  120.6 0.7 copy-done
  121.3 8.6 %all-to-all-start.1 = ((bf16[8,256,256]{2,1,0:T(8,128)(2,1)}), bf16[8,256,256]{2,1,0:T(8,128)(2,1)S(1)}, u32[]{:S(2)}, u32[]{:S(2)}) async-start(bf16[8,256,256]{2,1,0:T(8,128)(2,1)} %get-tuple-element.34), calls=%async_computation.1 | async-start | bytes 2097152 | tf_op jit(solution)/shard_map/all_to_all | solution.py:321
  129.9 1.9 collective-permute-start.9
  131.8 0.7 collective-permute-start.7
  132.5 0.8 collective-permute-done.9.x_ref
  133.3 0.7 copy-done.11
  134.0 1.8 pack_dq.1
  135.8 12.0 %collective-permute-start.10 = (bf16[224,256]{1,0:T(8,128)(2,1)}, bf16[224,256]{1,0:T(8,128)(2,1)S(1)}, u32[]{:S(2)}, u32[]{:S(2)}) collective-permute-start(bf16[224,256]{1,0:T(8,128)(2,1)} %get-tuple-element.30), channel_id=1, source_target_pairs={{506,0},{507,1},{508,2},{509,3},{510,4},{511,5},{504,6},{505,7},{4... | collective-permute-start | bytes 344072 | tf_op jit(solution)/shard_map/ppermute | solution.py:325
  147.9 2.9 %collective-permute-start.11 = (bf16[2,128,256]{2,1,0:T(8,128)(2,1)}, bf16[2,128,256]{2,1,0:T(8,128)(2,1)S(1)}, u32[]{:S(2)}, u32[]{:S(2)}) collective-permute-start(bf16[2,128,256]{2,1,0:T(8,128)(2,1)} %get-tuple-element.31), channel_id=1, source_target_pairs={{504,0},{505,1},{506,2},{507,3},{508,4},{509,5},{510,6},{511,7},{2... | collective-permute-start | bytes 393224 | tf_op jit(solution)/shard_map/ppermute | solution.py:325
  150.8 8.9 %collective-permute-start.12 = (bf16[2,128,256]{2,1,0:T(8,128)(2,1)}, bf16[2,128,256]{2,1,0:T(8,128)(2,1)S(1)}, u32[]{:S(2)}, u32[]{:S(2)}) collective-permute-start(bf16[2,128,256]{2,1,0:T(8,128)(2,1)} %get-tuple-element.32), channel_id=1, source_target_pairs={{508,0},{509,1},{510,2},{511,3},{504,4},{505,5},{506,6},{507,7},{6... | collective-permute-start | bytes 393224 | tf_op jit(solution)/shard_map/ppermute | solution.py:325
  159.7 2.1 collective-permute-start.13
  161.9 2.9 %collective-permute-start.8 = (bf16[32,256]{1,0:T(8,128)(2,1)S(1)}, bf16[32,256]{1,0:T(8,128)(2,1)S(1)}, u32[]{:S(2)}, u32[]{:S(2)}) collective-permute-start(bf16[32,256]{1,0:T(8,128)(2,1)S(1)} %broadcast_select_fusion.1), channel_id=1, source_target_pairs={{4,8},{5,9},{6,10},{7,11},{0,12},{1,13},{2,14},{3,15},{12,16},{13,... | collective-permute-start | bytes 49160 | tf_op jit(solution)/shard_map/ppermute | solution.py:327
  164.8 23.6 %all-to-all-done.1.in_ref = bf16[8,256,256]{2,1,0:T(8,128)(2,1)S(1)} async-done(((bf16[8,256,256]{2,1,0:T(8,128)(2,1)}), bf16[8,256,256]{2,1,0:T(8,128)(2,1)S(1)}, u32[]{:S(2)}, u32[]{:S(2)}) %all-to-all-start.1) | async-done | bytes 1048608 | tf_op jit(solution)/shard_map/all_to_all | solution.py:321
  188.4 1.0 copy-done.1
  189.3 2.7 %unpack_kv.1 = (f32[128,2048]{1,0:T(8,128)}, f32[128,2048]{1,0:T(8,128)}) custom-call(bf16[8,256,256]{2,1,0:T(8,128)(2,1)} %copy-done.1), custom_call_target="tpu_custom_call" | custom-call | tf_op jit(solution)/shard_map/unpack_kv/pallas_call | solution.py:277
  192.0 15.0 %collective-permute-done.10.rest_0_ = bf16[224,256]{1,0:T(8,128)(2,1)S(1)} collective-permute-done((bf16[224,256]{1,0:T(8,128)(2,1)}, bf16[224,256]{1,0:T(8,128)(2,1)S(1)}, u32[]{:S(2)}, u32[]{:S(2)}) %collective-permute-start.10) | collective-permute-done | bytes 114720 | tf_op jit(solution)/shard_map/ppermute | solution.py:325
  207.0 4.7 %collective-permute-done.11.rest_1_ = bf16[2,128,256]{2,1,0:T(8,128)(2,1)S(1)} collective-permute-done((bf16[2,128,256]{2,1,0:T(8,128)(2,1)}, bf16[2,128,256]{2,1,0:T(8,128)(2,1)S(1)}, u32[]{:S(2)}, u32[]{:S(2)}) %collective-permute-start.11) | collective-permute-done | bytes 131104 | tf_op jit(solution)/shard_map/ppermute | solution.py:325
  211.8 0.6 copy-done.3
  212.5 0.6 copy-done.7
  213.1 2.2 %unpack_q.1 = f32[128,2048]{1,0:T(8,128)} custom-call(s32[8]{0:T(128)} %stack.65.chunk_ref, bf16[32,256]{1,0:T(8,128)(2,1)} %copy-done.7, bf16[224,256]{1,0:T(8,128)(2,1)} %copy-done.6, bf16[2,128,256]{2,1,0:T(8,128)(2,1)} %copy-done.3, bf16[2,128,256]{2,1,0:T(8,128)(2,1)} %copy-done.4, bf16[2,128,256]{2,1,0:T(8,128)(2,1)} %copy-done.5), custom_call_target="tpu_custom_call" | custom-call | tf_op jit(solution)/shard_map/unpack_q/pallas_call | solution.py:259
  (34 shorter events, 0.3 us)
Async XLA Ops:
  2.9 112.6 %all-to-all-start = ((bf16[8,256,256]{2,1,0:T(8,128)(2,1)}), bf16[8,256,256]{2,1,0:T(8,128)(2,1)S(1)}, u32[]{:S(2)}, u32[]{:S(2)}) async-start(bf16[8,256,256]{2,1,0:T(8,128)(2,1)} %pack_kv.1), calls=%async_computation | async-start | bytes 2097152 | tf_op jit(solution)/shard_map/all_to_all | solution.py:300
  17.7 0.7 copy-start.8
  18.4 0.7 copy-start.9
  22.6 10.5 %collective-permute-start.2 = (bf16[4,272,256]{2,1,0:T(8,128)(2,1)}, bf16[4,272,256]{2,1,0:T(8,128)(2,1)S(1)}, u32[]{:S(2)}, u32[]{:S(2)}) collective-permute-start(bf16[4,272,256]{2,1,0:T(8,128)(2,1)} %pack_for_sibling.1), channel_id=1, source_target_pairs={{0,1},{1,0},{2,3},{3,2},{4,5},{5,4},{6,7},{7,6},{8,9},{9,8},{10,11... | collective-permute-start | bytes 1671176 | tf_op jit(solution)/shard_map/ppermute | solution.py:59
  25.4 40.7 %collective-permute-start = (bf16[128,256]{1,0:T(8,128)(2,1)S(1)}, bf16[128,256]{1,0:T(8,128)(2,1)S(1)}, u32[]{:S(2)}, u32[]{:S(2)}) collective-permute-start(bf16[128,256]{1,0:T(8,128)(2,1)S(1)} %constant_dynamic-slice_fusion), channel_id=1, source_target_pairs={{0,262},{1,263},{2,256},{3,257},{4,258},{5,259},{6,260},{7,261},{1... | collective-permute-start | bytes 196616 | tf_op jit(solution)/shard_map/ppermute | solution.py:303
  32.1 0.7 copy-start.10
  33.1 0.8 copy-start.2
  36.3 79.2 %collective-permute-start.3 = (bf16[400,256]{1,0:T(8,128)(2,1)}, bf16[400,256]{1,0:T(8,128)(2,1)S(1)}, u32[]{:S(2)}, u32[]{:S(2)}) collective-permute-start(bf16[400,256]{1,0:T(8,128)(2,1)} %get-tuple-element.23), channel_id=1, source_target_pairs={{0,506},{1,507},{2,508},{3,509},{4,510},{5,511},{6,504},{7,505},{8... | collective-permute-start | bytes 614408 | tf_op jit(solution)/shard_map/ppermute | solution.py:312
  46.8 68.7 %collective-permute-start.4 = (bf16[528,256]{1,0:T(8,128)(2,1)}, bf16[528,256]{1,0:T(8,128)(2,1)S(1)}, u32[]{:S(2)}, u32[]{:S(2)}) collective-permute-start(bf16[528,256]{1,0:T(8,128)(2,1)} %get-tuple-element.24), channel_id=1, source_target_pairs={{0,504},{1,505},{2,506},{3,507},{4,508},{5,509},{6,510},{7,511},{8... | collective-permute-start | bytes 811016 | tf_op jit(solution)/shard_map/ppermute | solution.py:312
  49.3 66.2 %collective-permute-start.5 = (bf16[528,256]{1,0:T(8,128)(2,1)}, bf16[528,256]{1,0:T(8,128)(2,1)S(1)}, u32[]{:S(2)}, u32[]{:S(2)}) collective-permute-start(bf16[528,256]{1,0:T(8,128)(2,1)} %get-tuple-element.25), channel_id=1, source_target_pairs={{0,508},{1,509},{2,510},{3,511},{4,504},{5,505},{6,506},{7,507},{8... | collective-permute-start | bytes 811016 | tf_op jit(solution)/shard_map/ppermute | solution.py:312
  57.1 58.4 %collective-permute-start.6 = (bf16[528,256]{1,0:T(8,128)(2,1)}, bf16[528,256]{1,0:T(8,128)(2,1)S(1)}, u32[]{:S(2)}, u32[]{:S(2)}) collective-permute-start(bf16[528,256]{1,0:T(8,128)(2,1)} %get-tuple-element.26), channel_id=1, source_target_pairs={{0,510},{1,511},{2,504},{3,505},{4,506},{5,507},{6,508},{7,509},{8... | collective-permute-start | bytes 811016 | tf_op jit(solution)/shard_map/ppermute | solution.py:312
  66.9 48.6 %collective-permute-start.1 = (bf16[128,256]{1,0:T(8,128)(2,1)S(1)}, bf16[128,256]{1,0:T(8,128)(2,1)S(1)}, u32[]{:S(2)}, u32[]{:S(2)}) collective-permute-start(bf16[128,256]{1,0:T(8,128)(2,1)S(1)} %broadcast_select_fusion), channel_id=1, source_target_pairs={{8,4},{9,5},{10,6},{11,7},{12,0},{13,1},{14,2},{15,3},{16,12},{17,... | collective-permute-start | bytes 196616 | tf_op jit(solution)/shard_map/ppermute | solution.py:311
  120.6 0.7 copy-start
  121.3 67.0 %all-to-all-start.1 = ((bf16[8,256,256]{2,1,0:T(8,128)(2,1)}), bf16[8,256,256]{2,1,0:T(8,128)(2,1)S(1)}, u32[]{:S(2)}, u32[]{:S(2)}) async-start(bf16[8,256,256]{2,1,0:T(8,128)(2,1)} %get-tuple-element.34), calls=%async_computation.1 | async-start | bytes 2097152 | tf_op jit(solution)/shard_map/all_to_all | solution.py:321
  129.9 3.4 %collective-permute-start.9 = (bf16[4,128,256]{2,1,0:T(8,128)(2,1)S(1)}, bf16[4,128,256]{2,1,0:T(8,128)(2,1)S(1)}, u32[]{:S(2)}, u32[]{:S(2)}) collective-permute-start(bf16[4,128,256]{2,1,0:T(8,128)(2,1)S(1)} %get-tuple-element.29), channel_id=1, source_target_pairs={{0,1},{1,0},{2,3},{3,2},{4,5},{5,4},{6,7},{7,6},{8,9},{9,8},{10,11... | collective-permute-start | bytes 786440 | tf_op jit(solution)/shard_map/ppermute | solution.py:59
  131.8 30.1 %collective-permute-start.7 = (bf16[32,256]{1,0:T(8,128)(2,1)S(1)}, bf16[32,256]{1,0:T(8,128)(2,1)S(1)}, u32[]{:S(2)}, u32[]{:S(2)}) collective-permute-start(bf16[32,256]{1,0:T(8,128)(2,1)S(1)} %get-tuple-element.27), channel_id=1, source_target_pairs={{506,252},{507,253},{508,254},{509,255},{510,248},{511,249},{504,2... | collective-permute-start | bytes 49160 | tf_op jit(solution)/shard_map/ppermute | solution.py:323
  133.3 0.7 copy-start.11
  135.8 71.2 %collective-permute-start.10 = (bf16[224,256]{1,0:T(8,128)(2,1)}, bf16[224,256]{1,0:T(8,128)(2,1)S(1)}, u32[]{:S(2)}, u32[]{:S(2)}) collective-permute-start(bf16[224,256]{1,0:T(8,128)(2,1)} %get-tuple-element.30), channel_id=1, source_target_pairs={{506,0},{507,1},{508,2},{509,3},{510,4},{511,5},{504,6},{505,7},{4... | collective-permute-start | bytes 344072 | tf_op jit(solution)/shard_map/ppermute | solution.py:325
  147.9 63.8 %collective-permute-start.11 = (bf16[2,128,256]{2,1,0:T(8,128)(2,1)}, bf16[2,128,256]{2,1,0:T(8,128)(2,1)S(1)}, u32[]{:S(2)}, u32[]{:S(2)}) collective-permute-start(bf16[2,128,256]{2,1,0:T(8,128)(2,1)} %get-tuple-element.31), channel_id=1, source_target_pairs={{504,0},{505,1},{506,2},{507,3},{508,4},{509,5},{510,6},{511,7},{2... | collective-permute-start | bytes 393224 | tf_op jit(solution)/shard_map/ppermute | solution.py:325
  150.8 60.9 %collective-permute-start.12 = (bf16[2,128,256]{2,1,0:T(8,128)(2,1)}, bf16[2,128,256]{2,1,0:T(8,128)(2,1)S(1)}, u32[]{:S(2)}, u32[]{:S(2)}) collective-permute-start(bf16[2,128,256]{2,1,0:T(8,128)(2,1)} %get-tuple-element.32), channel_id=1, source_target_pairs={{508,0},{509,1},{510,2},{511,3},{504,4},{505,5},{506,6},{507,7},{6... | collective-permute-start | bytes 393224 | tf_op jit(solution)/shard_map/ppermute | solution.py:325
  159.7 52.0 %collective-permute-start.13 = (bf16[2,128,256]{2,1,0:T(8,128)(2,1)}, bf16[2,128,256]{2,1,0:T(8,128)(2,1)S(1)}, u32[]{:S(2)}, u32[]{:S(2)}) collective-permute-start(bf16[2,128,256]{2,1,0:T(8,128)(2,1)} %get-tuple-element.33), channel_id=1, source_target_pairs={{510,0},{511,1},{504,2},{505,3},{506,4},{507,5},{508,6},{509,7},{0... | collective-permute-start | bytes 393224 | tf_op jit(solution)/shard_map/ppermute | solution.py:325
  161.9 49.8 %collective-permute-start.8 = (bf16[32,256]{1,0:T(8,128)(2,1)S(1)}, bf16[32,256]{1,0:T(8,128)(2,1)S(1)}, u32[]{:S(2)}, u32[]{:S(2)}) collective-permute-start(bf16[32,256]{1,0:T(8,128)(2,1)S(1)} %broadcast_select_fusion.1), channel_id=1, source_target_pairs={{4,8},{5,9},{6,10},{7,11},{0,12},{1,13},{2,14},{3,15},{12,16},{13,... | collective-permute-start | bytes 49160 | tf_op jit(solution)/shard_map/ppermute | solution.py:327
  188.4 1.0 copy-start.1
  207.0 4.7 %copy-start.6 = (bf16[224,256]{1,0:T(8,128)(2,1)}, bf16[224,256]{1,0:T(8,128)(2,1)S(1)}, u32[]{:S(2)}) copy-start(bf16[224,256]{1,0:T(8,128)(2,1)S(1)} %collective-permute-done.10.rest_0_) | copy-start | bytes 344068
  211.7 0.7 copy-start.3
  211.7 0.7 copy-start.4
  211.7 0.7 copy-start.5
  212.5 0.6 copy-start.7
